TPU v7x, 32 devices: a whole 2x2x4 slice. The times are simulated.
32 devices in a mesh: gx: 4 (over y, core), gy: 8 (over z, x).
Axes of the slice: x: 2, y: 2, z: 4, core: 2. Of those that a mesh axis runs over, the one named last changes fastest.
Arguments:
- tokens: bfloat16 [16384, 2048], P('gy', 'gx'), may hold values from -6 to 6
- query_weight: bfloat16 [2048, 2048], P('gy', 'gx'), may hold values from -0.125 to 0.125
- key_weight: bfloat16 [2048, 2048], P('gy', 'gx'), may hold values from -0.125 to 0.125
- value_weight: bfloat16 [2048, 2048], P('gy', 'gx'), may hold values from -0.125 to 0.125
- output_weight: bfloat16 [2048, 2048], P('gx', 'gy'), may hold values from -0.125 to 0.125
- gate_weight: bfloat16 [2048, 8192], P('gy', 'gx'), may hold values from -0.125 to 0.125
- up_weight: bfloat16 [2048, 8192], P('gy', 'gx'), may hold values from -0.125 to 0.125
- down_weight: bfloat16 [8192, 2048], P('gx', 'gy'), may hold values from -0.0625 to 0.0625
- query_gain: float32 [2048], P('gx'), may hold values from 0.25 to 1.75
- key_gain: float32 [2048], P('gx'), may hold values from 0.25 to 1.75
- attn_gain: float32 [2048], P('gx'), may hold values from 0.25 to 1.75
- mlp_gain: float32 [2048], P('gx'), may hold values from 0.25 to 1.75
- seq_ids: int32 [8, 2048], P('gy'), may hold values from 0 to 3, never falling along the last dimension, each value on 1 to 1024 neighbouring positions
- out_grad: bfloat16 [16384, 2048], P('gy', 'gx'), may hold values from -6 to 6
Outputs:
- result: bfloat16 [16384, 2048], P('gy', 'gx')
- token_grad: float32 [16384, 2048], P('gy', 'gx')
- query_weight_grad: float32 [2048, 2048], P('gy', 'gx')
- key_weight_grad: float32 [2048, 2048], P('gy', 'gx')
- value_weight_grad: float32 [2048, 2048], P('gy', 'gx')
- output_weight_grad: float32 [2048, 2048], P('gx', 'gy')
- gate_weight_grad: float32 [2048, 8192], P('gy', 'gx')
- up_weight_grad: float32 [2048, 8192], P('gy', 'gx')
- down_weight_grad: float32 [8192, 2048], P('gx', 'gy')
- query_gain_grad: float32 [2048], P('gx')
- key_gain_grad: float32 [2048], P('gx')
- attn_gain_grad: float32 [2048], P('gx')
- mlp_gain_grad: float32 [2048], P('gx')
Inputs may be any that keep to these rules, and one draw needn't show every extreme that they name: `seq_ids`: in each row of 2048 tokens the numbers never fall, every number appears, each sequence has 1 to 1024 tokens and one has exactly 1024.
All inputs are finite; a program needn't handle non-finite values.
Results may differ from a plain program's by a relative error of at most 0.024.
Values may be sent and summed in bfloat16 or wider, within the bound.
A program may use at most 320 MiB of HBM per device.

v0:
```python
import math

import jax
import jax.numpy as jnp
from jax import lax
from jax.experimental import pallas as pl
from jax.experimental.pallas import tpu as pltpu
from jax.sharding import PartitionSpec as P

D = 2048
HEAD = 128
MAX_LEN = 1024
SEGS = 4


EPS = 1e-06
THETA = 500000.0
NEGATIVE = -1e30


MESH = pl.DeviceIdType.MESH
HBM = pl.BlockSpec(memory_space=pltpu.HBM)
VMEM = pl.BlockSpec(memory_space=pltpu.VMEM)
LOW = jnp.bfloat16
WIDE = jnp.float32
MIB = 1 << 20
LAG = 2
STATS = 128


def core_here():
    return lax.rem(lax.axis_index("gx"), 2)


def chip_here():
    return lax.div(lax.axis_index("gx"), 2)


def other_core():
    return lax.axis_index("gx") + 1 - 2 * core_here()


def peer_at(shift):
    return lax.rem(lax.axis_index("gx") + 2 * shift, lax.axis_size("gx"))


def rank_at(shift):
    return lax.rem(lax.axis_index("gx") + shift, lax.axis_size("gx"))


def block_at(shift):
    return lax.rem(lax.axis_index("gy") + shift, lax.axis_size("gy"))


def ring_place():
    count = lax.axis_size("gy")
    index = lax.axis_index("gy")
    row, side = lax.div(index, 2), lax.rem(index, 2)
    return side * row + (1 - side) * (count - 1 - row)


def ring_device(place):
    count = lax.axis_size("gy")
    place = lax.rem(place + 2 * count, count)
    back = lax.div(place, count // 2)
    row = (1 - back) * place + back * (count - 1 - place)
    return 2 * row + 1 - back


def greet(gx, ring, all_blocks=False):
    barrier = pltpu.get_barrier_semaphore()
    partners = []
    if all_blocks:
        partners += [{"gy": block_at(k)} for k in range(1, lax.axis_size("gy"))]
    if gx == "all":
        partners += [{"gx": rank_at(k)} for k in range(1, lax.axis_size("gx"))]
    elif gx:
        partners.append({"gx": other_core()})
        partners += [{"gx": peer_at(k)} for k in range(1, lax.axis_size("gx") // 2)]
    if ring:
        place = ring_place()
        partners += [{"gy": ring_device(place + 1)}, {"gy": ring_device(place - 1)}]
    for partner in partners:
        pl.semaphore_signal(barrier, inc=1, device_id=partner, device_id_type=MESH)
    pl.semaphore_wait(barrier, len(partners))


def remote(source, target, send, recv, device):
    return pltpu.make_async_remote_copy(
        src_ref=source,
        dst_ref=target,
        send_sem=send,
        recv_sem=recv,
        device_id=device,
        device_id_type=MESH,
    )


def loop(count, body):
    def step(index, carry):
        body(index)
        return carry

    lax.fori_loop(0, count, step, 0)


def aligned(value, factor):
    return pl.multiple_of(value, factor)


class RingGather:
    def __init__(self, sources, slot, spill, parts, send, recv, local, spilled):
        self.sources, self.slot, self.spill, self.parts = sources, slot, spill, parts
        self.send, self.recv, self.local, self.spilled = send, recv, local, spilled
        self.count = lax.axis_size("gy")

    @staticmethod
    def scratch(parts):
        count = lax.axis_size("gy")
        return [
            pltpu.SemaphoreType.DMA((count - 1, 2, parts)),
            pltpu.SemaphoreType.DMA((count - 1, 2, parts)),
            pltpu.SemaphoreType.DMA((2, parts)),
            pltpu.SemaphoreType.DMA((count, 2, parts)),
        ]

    def spill_copy(self, way, step, part):
        place = ring_place()
        owner = ring_device(place - (1 - 2 * way) * step)
        return pltpu.make_async_copy(
            self.slot(way, owner, part),
            self.spill(way, owner, part),
            self.spilled.at[step, way, part],
        )

    def copy(self, way, step, part, behind):
        place = ring_place()
        sign = 1 - 2 * way
        spot = self.slot(way, ring_device(place - sign * (step + behind)), part)
        return remote(
            spot,
            spot,
            self.send.at[step, way, part],
            self.recv.at[step, way, part],
            {"gy": ring_device(place + sign)},
        )

    def begin(self):
        place = [
            pltpu.make_async_copy(
                self.sources(way, part),
                self.slot(way, lax.axis_index("gy"), part),
                self.local.at[way, part],
            )
            for way in range(2)
            for part in range(self.parts)
        ]
        for item in place:
            item.start()
        for item in place:
            item.wait()
        for part in range(self.parts):
            for way in range(2):
                self.copy(way, 0, part, 0).start()
                self.spill_copy(way, 0, part).start()

    @property
    def events(self):
        return (self.count - 2) * self.parts

    def event(self, index):
        step = 1 + lax.div(index, self.parts)
        for part in range(self.parts):

            @pl.when(lax.rem(index, self.parts) == part)
            def _():
                for way in range(2):
                    self.copy(way, step - 1, part, 1).wait_recv()
                    self.copy(way, step, part, 0).start()
                    self.spill_copy(way, step, part).start()

    def end(self):
        for part in range(self.parts):
            for way in range(2):
                self.copy(way, self.count - 2, part, 1).wait_recv()
                self.spill_copy(way, self.count - 1, part).start()

        def drain(step):
            for part in range(self.parts):
                for way in range(2):
                    self.copy(way, step, part, 0).wait_send()

        loop(self.count - 1, drain)

    def settle(self):
        def drain(step):
            for part in range(self.parts):
                for way in range(2):
                    self.spill_copy(way, step, part).wait()

        loop(self.count, drain)


class RingScatter:
    def __init__(self, product, total, sums, land, send, recv, credit, slots, parts):
        self.product, self.total, self.sums, self.land = product, total, sums, land
        self.send, self.recv, self.credit = send, recv, credit
        self.slots, self.parts = slots, parts
        self.count = lax.axis_size("gy")
        self.rows = total.shape[1] // parts

    @staticmethod
    def scratch(rows, columns, slots, parts):
        count = lax.axis_size("gy")
        return [
            pltpu.VMEM((2, rows, columns), WIDE),
            pltpu.VMEM((2, rows, columns), LOW),
            pltpu.VMEM((slots, 2, rows, columns), LOW),
            pltpu.SemaphoreType.DMA((count - 1, 2, parts)),
            pltpu.SemaphoreType.DMA((count - 1, 2, parts)),
            pltpu.SemaphoreType.REGULAR((2, parts)),
        ]

    def copy(self, way, step, part):
        place = ring_place()
        rows = pl.ds(aligned(part * self.rows, self.rows), self.rows)
        return remote(
            self.sums.at[way, rows],
            self.land.at[lax.rem(step, self.slots), way, rows],
            self.send.at[step, way, part],
            self.recv.at[step, way, part],
            {"gy": ring_device(place + 1 - 2 * way)},
        )

    def owner(self, way, step):
        sign = 1 - 2 * way
        return ring_device(ring_place() - sign * (1 + step))

    @property
    def events(self):
        return self.count * self.parts

    def event(self, index):
        step, part = lax.div(index, self.parts), lax.rem(index, self.parts)
        last = self.count - 1
        tile = min(self.rows, 32)

        @pl.when(part == 0)
        def _():
            for way in range(2):
                self.product(way, step)

        for way in range(2):
            base = part * self.rows

            slot = lax.rem(step - 1 + self.slots, self.slots)

            def over(body):
                @pl.loop(0, self.rows // tile)
                def _(index):
                    body(pl.ds(aligned(base + index * tile, tile), tile))

            @pl.when(step >= 1)
            def _():
                self.copy(way, step - 1, part).wait_recv()

            @pl.when((step >= 1) & (step < last))
            def _():
                self.copy(way, step - 1, part).wait_send()

            @pl.when(step == 0)
            def _():
                def first(rows):
                    self.sums[way, rows] = self.total[way, rows].astype(LOW)

                over(first)

            @pl.when((step >= 1) & (step < last))
            def _():
                def more(rows):
                    summed = self.total[way, rows] + self.land[slot, way, rows].astype(WIDE)
                    self.sums[way, rows] = summed.astype(LOW)

                over(more)

            @pl.when(step == last)
            def _():
                def final(rows):
                    self.total[way, rows] += self.land[slot, way, rows].astype(WIDE)

                over(final)

            @pl.when((step >= 1) & (step - 1 + self.slots < last))
            def _():
                upstream = ring_device(ring_place() - (1 - 2 * way))
                pl.semaphore_signal(
                    self.credit.at[way, part],
                    inc=1,
                    device_id={"gy": upstream},
                    device_id_type=MESH,
                )

            @pl.when(step < last)
            def _():
                @pl.when(step >= self.slots)
                def _():
                    pl.semaphore_wait(self.credit.at[way, part], 1)

                self.copy(way, step, part).start()

    def end(self):
        for part in range(self.parts):
            for way in range(2):
                self.copy(way, self.count - 2, part).wait_send()


class Reduce:
    def __init__(self, refs, cross_land, rows, width, scatter):
        (
            self.keep,
            self.core_send,
            self.core_land,
            self.cross,
            self.cross_stage,
            self.raw,
            self.core_sems,
            self.cross_send_sems,
            self.cross_recv_sems,
            self.stage_sems,
        ) = refs
        self.cross_land = cross_land
        self.rows, self.width, self.scatter = rows, width, scatter
        self.chips = lax.axis_size("gx") // 2

    @staticmethod
    def scratch(rows, chunks, width, scatter):
        chips = lax.axis_size("gx") // 2
        half = chips * width
        part = width if scatter else half
        return [
            pltpu.VMEM((1, rows, half), LOW),
            pltpu.VMEM((2, rows, half), LOW),
            pltpu.VMEM((2, rows, half), LOW),
            pltpu.VMEM((LAG + 2, chips, rows, width) if scatter else (LAG + 2, rows, half), LOW),
            pltpu.VMEM((chips - 1, rows, part), LOW),
            pltpu.VMEM((rows, part), WIDE),
            pltpu.SemaphoreType.DMA((2, chunks)),
            pltpu.SemaphoreType.DMA((chips - 1, chunks)),
            pltpu.SemaphoreType.DMA((chips - 1, chunks)),
            pltpu.SemaphoreType.DMA((chips,)),
        ]

    @staticmethod
    def landing(rows, chunks, width, scatter):
        chips = lax.axis_size("gx") // 2
        half = chips * width
        part = width if scatter else half
        return [jax.ShapeDtypeStruct((chips - 1, chunks, rows, part), LOW)]

    def core_copy(self, chunk):
        return remote(
            self.core_send.at[lax.rem(chunk, 2)],
            self.core_land.at[lax.rem(chunk, 2)],
            self.core_sems.at[0, chunk],
            self.core_sems.at[1, chunk],
            {"gx": other_core()},
        )

    def cross_copy(self, shift, chunk):
        source = self.cross.at[lax.rem(chunk, LAG + 2)]
        if self.scatter:
            block = lax.rem(chip_here() + shift, self.chips)
            source = source.at[block]
        return remote(
            source,
            self.cross_land.at[shift - 1, chunk],
            self.cross_send_sems.at[shift - 1, chunk],
            self.cross_recv_sems.at[shift - 1, chunk],
            {"gx": peer_at(shift)},
        )

    def produce(self, chunk, dot):
        @pl.when(chunk >= 2)
        def _():
            self.core_copy(chunk - 2).wait_send()

        slot = lax.rem(chunk, 2)
        core = core_here()
        for chip in range(self.chips):
            place = aligned((2 * chip + 1 - core) * self.width, self.width)
            self.core_send[slot, :, chip * self.width : (chip + 1) * self.width] = dot(
                place
            ).astype(LOW)
        self.core_copy(chunk).start()
        for chip in range(self.chips):
            place = aligned((2 * chip + core) * self.width, self.width)
            self.keep[0, :, chip * self.width : (chip + 1) * self.width] = dot(
                place
            ).astype(LOW)

    def core_sum(self, chunk):
        slot, place = lax.rem(chunk, 2), lax.rem(chunk, LAG + 2)
        self.core_copy(chunk).wait_recv()

        @pl.when(chunk >= LAG + 2)
        def _():
            for shift in range(1, self.chips):
                self.cross_copy(shift, chunk - LAG - 2).wait_send()

        @pl.loop(0, self.rows // 32)
        def _(index):
            rows = pl.ds(aligned(index * 32, 32), 32)
            total = self.keep[0, rows].astype(WIDE) + self.core_land[slot, rows].astype(WIDE)
            if self.scatter:
                for chip in range(self.chips):
                    columns = slice(chip * self.width, (chip + 1) * self.width)
                    self.cross[place, chip, rows] = total[:, columns].astype(LOW)
            else:
                self.cross[place, rows] = total.astype(LOW)

        for shift in range(1, self.chips):
            self.cross_copy(shift, chunk).start()

    def cross_stage_copy(self, shift, chunk):
        return pltpu.make_async_copy(
            self.cross_land.at[shift - 1, chunk],
            self.cross_stage.at[shift - 1],
            self.stage_sems.at[shift],
        )

    def cross_fetch(self, chunk):
        for shift in range(1, self.chips):
            self.cross_copy(shift, chunk).wait_recv()
            self.cross_stage_copy(shift, chunk).start()

    def cross_sum(self, chunk):
        place = lax.rem(chunk, LAG + 2)
        for shift in range(1, self.chips):
            self.cross_stage_copy(shift, chunk).wait()

        @pl.loop(0, self.rows // 32)
        def _(index):
            rows = pl.ds(aligned(index * 32, 32), 32)
            if self.scatter:
                total = self.cross[place, chip_here(), rows].astype(WIDE)
            else:
                total = self.cross[place, rows].astype(WIDE)
            for shift in range(1, self.chips):
                total = total + self.cross_stage[shift - 1, rows].astype(WIDE)
            self.raw[rows] = total

    def end(self, chunks):
        for chunk in (chunks - 2, chunks - 1):
            self.core_copy(chunk).wait_send()
        for chunk in range(chunks - LAG - 2, chunks):
            for shift in range(1, self.chips):
                self.cross_copy(shift, chunk).wait_send()


class Stats:
    def __init__(self, mine, land, sems):
        self.mine, self.land, self.sems = mine, land, sems

    @staticmethod
    def scratch(rows, chunks):
        return [
            pltpu.VMEM((2, rows, STATS), WIDE),
            pltpu.VMEM((chunks, rows, STATS), WIDE),
            pltpu.SemaphoreType.DMA((2, chunks)),
        ]

    def copy(self, chunk):
        return remote(
            self.mine.at[lax.rem(chunk, 2)],
            self.land.at[chunk],
            self.sems.at[0, chunk],
            self.sems.at[1, chunk],
            {"gx": other_core()},
        )

    def clear(self, chunk):
        @pl.when(chunk >= 2)
        def _():
            self.copy(chunk - 2).wait_send()

    def put(self, chunk, rows, first, second):
        lane = lax.broadcasted_iota(jnp.int32, (first.shape[0], STATS), 1)
        self.mine[lax.rem(chunk, 2), rows] = jnp.where(lane < STATS // 2, first, second)

    def get(self, chunk, rows):
        total = self.mine[lax.rem(chunk, 2), rows] + self.land[chunk, rows]
        return (total[:, :1], total[:, STATS // 2 : STATS // 2 + 1])

    def end(self, chunks):
        for chunk in (chunks - 2, chunks - 1):
            self.copy(chunk).wait_send()


class Spread:
    def __init__(self, buffer, whole, local, send, recv, rows, width):
        self.buffer, self.whole = buffer, whole
        self.local, self.send, self.recv = local, send, recv
        self.rows, self.width = rows, width
        self.chips = lax.axis_size("gx") // 2

    @staticmethod
    def scratch(rows, chunks, width):
        chips = lax.axis_size("gx") // 2
        return [
            pltpu.VMEM((2, chips, rows, width), LOW),
            pltpu.SemaphoreType.DMA((2, chips)),
            pltpu.SemaphoreType.DMA((chunks, chips)),
            pltpu.SemaphoreType.DMA((chunks, chips)),
        ]

    def pair(self, chunk, chip, core):
        slot = lax.rem(chunk, 2)
        source = self.buffer.at[slot, chip]
        rows = pl.ds(aligned(chunk * self.rows, self.rows), self.rows)
        rank = 2 * chip + core
        if len(self.whole.shape) == 3:
            target = self.whole.at[rank, rows]
        else:
            columns = pl.ds(aligned(rank * self.width, self.width), self.width)
            target = self.whole.at[rows, columns]
        here = pltpu.make_async_copy(source, target, self.local.at[slot, chip])
        away = remote(
            source,
            target,
            self.send.at[chunk, chip],
            self.recv.at[chunk, chip],
            {"gx": other_core()},
        )
        return (here, away)

    def put(self, chunk, rows, values):
        for chip in range(self.chips):
            columns = slice(chip * self.width, (chip + 1) * self.width)
            self.buffer[lax.rem(chunk, 2), chip, rows] = values[:, columns].astype(LOW)

    def clear(self, chunk):
        @pl.when(chunk >= 2)
        def _():
            self.settle(chunk - 2)

    def settle(self, chunk):
        for chip in range(self.chips):
            here, away = self.pair(chunk, chip, core_here())
            here.wait()
            away.wait_send()

    def go(self, chunk):
        for chip in range(self.chips):
            here, away = self.pair(chunk, chip, core_here())
            here.start()
            away.start()

    def end(self, chunks):
        for chunk in (chunks - 2, chunks - 1):
            self.settle(chunk)

        def arrive(chunk):
            for chip in range(self.chips):
                self.pair(chunk, chip, 1 - core_here())[1].wait_recv()

        loop(chunks, arrive)


def row_slice(chunk, rows):
    return pl.ds(aligned(chunk * rows, rows), rows)


def core_blocks(source, chunk, rows, width, buffer, sems):
    return [
        pltpu.make_async_copy(
            source.at[2 * chip + core_here(), row_slice(chunk, rows)],
            buffer.at[:, chip * width : (chip + 1) * width],
            sems.at[chip],
        )
        for chip in range(lax.axis_size("gx") // 2)
    ]


def all_blocks(source, rows, width, buffer, sems):
    return [
        pltpu.make_async_copy(
            source.at[rank] if rows is None else source.at[rank, rows],
            buffer.at[:, rank * width : (rank + 1) * width],
            sems.at[rank],
        )
        for rank in range(source.shape[0])
    ]


def tiles(rows, body):
    @pl.loop(0, rows // 32)
    def _(index):
        body(pl.ds(aligned(index * 32, 32), 32))


def schedule(chunks, reduce, multiply, fetch, sums, finish, event=None, events=0, prepare=None):
    steps = chunks + 1 + LAG

    def iteration(step):
        if event is not None:
            low = lax.div(step * events, steps)
            high = lax.div((step + 1) * events, steps)

            def some(index, carry):
                event(index)
                return carry

            lax.fori_loop(low, high, some, 0)

        @pl.when((step >= LAG) & (step < chunks + LAG))
        def _():
            reduce.cross_fetch(step - LAG)

        @pl.when(step >= LAG)
        def _():
            fetch(step - LAG)

        @pl.when(step < chunks)
        def _():
            if prepare is not None:
                prepare(step)
            reduce.produce(step, lambda place: multiply(step, place))
            reduce.core_sum(step)

        @pl.when(step >= 1 + LAG)
        def _():
            finish(step - 1 - LAG)

        @pl.when((step >= LAG) & (step < chunks + LAG))
        def _():
            reduce.cross_sum(step - LAG)
            sums(step - LAG)

    loop(steps, iteration)


def take(refs, counts):
    groups, start = [], 0
    for count in counts:
        groups.append(refs[start : start + count])
        start += count
    return groups


class Columns:
    def __init__(self, source, shard, left, turned, sem):
        self.source, self.shard = source, shard
        self.left, self.turned, self.sem = left, turned, sem

    @staticmethod
    def scratch(length, shard):
        return [
            pltpu.VMEM((length, shard), LOW),
            pltpu.VMEM((shard, length), LOW),
            pltpu.SemaphoreType.DMA((1,)),
        ]

    def copy(self, owner):
        each = self.source.shape[2] // self.shard
        at = pl.ds(aligned(lax.rem(owner, each) * self.shard, self.shard), self.shard)
        source = self.source.at[lax.div(owner, each), :, at]
        return pltpu.make_async_copy(source, self.left, self.sem.at[0])

    def take(self, ring, way, step):
        self.copy(ring.owner(way, step)).wait()
        self.turned[...] = self.left[...].T
        if way == 0:
            self.copy(ring.owner(1, step)).start()
        else:

            @pl.when(step + 1 < ring.count)
            def _():
                self.copy(ring.owner(0, step + 1)).start()


def attn_out(
    attended, weight, gain, tokens, out_grad, gate_shard, up_shard, down_shard, collective
):
    length, width = attended.shape
    chips = lax.axis_size("gx") // 2
    half = chips * width
    count = lax.axis_size("gy")
    chunks = count
    rows = length // chunks
    hidden = gate_shard.shape[1]
    inner = down_shard.shape[0]
    shard = gate_shard.shape[0]
    part_rows = shard // 2
    side = inner // 2
    down_columns = down_shard.shape[1]

    groups = [
        Reduce.scratch(rows, chunks, width, False),
        Stats.scratch(rows, chunks),
        Spread.scratch(rows, chunks, width),
        RingGather.scratch(3),
        [
            pltpu.VMEM((rows, half), LOW),
            pltpu.VMEM((2, rows, half), WIDE),
            pltpu.VMEM((2, rows, half), LOW),
            pltpu.SemaphoreType.DMA((chips,)),
            pltpu.SemaphoreType.DMA((2,)),
            pltpu.SemaphoreType.DMA((2,)),
            pltpu.SemaphoreType.DMA((2,)),
            pltpu.SemaphoreType.DMA((chips - 1, chunks, 2)),
        ],
        [
            pltpu.VMEM((2, D, hidden), LOW),
            pltpu.VMEM((count, inner, down_columns), LOW),
            pltpu.VMEM((chips, length, width), LOW),
        ],
    ]

    def kernel(*refs):
        ins, outs, *scratch = take(refs, [8, 8] + [len(g) for g in groups])
        attended, weight, gain, tokens, out_grad, gate_shard, up_shard, down_shard = ins
        raw_out, mixed_out, low_out, gate_full, up_full, down_full, upstream = outs[:7]
        cross_land = outs[7]
        reduce = Reduce(scratch[0], cross_land, rows, width, False)
        stats = Stats(*scratch[1])
        buffer, local, send, recv = scratch[2]
        spread = Spread(buffer, low_out, local, send, recv, rows, width)
        token_buf, mixed_buf, raw_buf = scratch[4][:3]
        token_sems, mixed_sems, raw_sems, own_sem, up_sems = scratch[4][3:]
        held, held_down, up_land = scratch[5]
        shards_here = (gate_shard, up_shard)

        def place_in(full, down):
            def slot(way, owner, part):
                if part == 2:
                    return down.at[owner, way * side : (way + 1) * side]
                base = owner * shard + part * part_rows
                return full[way].at[pl.ds(aligned(base, part_rows), part_rows)]

            return slot

        slot = place_in((held.at[0], held.at[1]), held_down)
        spill = place_in((gate_full, up_full), down_full)

        def source(way, part):
            if part == 2:
                return down_shard.at[way * side : (way + 1) * side]
            return shards_here[way].at[part * part_rows : (part + 1) * part_rows]

        ring = RingGather(source, slot, spill, 3, *scratch[3])
        own = pltpu.make_async_copy(out_grad, up_land.at[chip_here()], own_sem.at[0])
        up_spill = pltpu.make_async_copy(up_land, upstream, own_sem.at[1])

        def crossings(chunk):
            at = row_slice(chunk, rows)
            return [
                remote(
                    up_land.at[chip_here(), at],
                    up_land.at[chip_here(), at],
                    up_sems.at[shift - 1, chunk, 0],
                    up_sems.at[shift - 1, chunk, 1],
                    {"gx": peer_at(shift)},
                )
                for shift in range(1, chips)
            ]

        own.start()
        greet(True, True)
        ring.begin()
        own.wait()

        def multiply(chunk, place):
            return jnp.dot(
                attended[row_slice(chunk, rows)],
                weight[:, pl.ds(place, width)],
                preferred_element_type=WIDE,
            )

        def prepare(chunk):
            for item in crossings(chunk):
                item.start()

        def token_copies(chunk):
            return core_blocks(tokens, chunk, rows, width, token_buf, token_sems)

        def fetch(chunk):
            @pl.when(chunk >= 1)
            def _():
                for item in token_copies(chunk - 1):
                    item.start()

        def mixed_copy(chunk):
            slot = lax.rem(chunk, 2)
            return pltpu.make_async_copy(
                mixed_buf.at[slot, :, pl.ds(aligned(chip_here() * width, width), width)],
                mixed_out.at[row_slice(chunk, rows)],
                mixed_sems.at[slot],
            )

        def raw_copy(chunk):
            slot = lax.rem(chunk, 2)
            return pltpu.make_async_copy(
                raw_buf.at[slot], raw_out.at[row_slice(chunk, rows)], raw_sems.at[slot]
            )

        def sums(chunk):
            stats.clear(chunk)

            @pl.when(chunk >= 2)
            def _():
                raw_copy(chunk - 2).wait()

            def tile(at):
                raw = reduce.raw[at]
                raw_buf[lax.rem(chunk, 2), at] = raw.astype(LOW)
                squares = jnp.sum(raw * raw, axis=1, keepdims=True)
                stats.put(chunk, at, squares, squares)

            tiles(rows, tile)
            stats.copy(chunk).start()
            raw_copy(chunk).start()

        def finish(chunk):
            slot = lax.rem(chunk, 2)
            for item in token_copies(chunk):
                item.wait()
            stats.copy(chunk).wait_recv()
            spread.clear(chunk)

            @pl.when(chunk >= 2)
            def _():
                mixed_copy(chunk - 2).wait()

            def tile(at):
                squares, _ = stats.get(chunk, at)
                factor = lax.rsqrt(squares / D + EPS)
                mixed = token_buf[at].astype(WIDE) + reduce.raw[at] * factor * gain[...]
                mixed_buf[slot, at] = mixed
                spread.put(chunk, at, mixed)

            tiles(rows, tile)
            spread.go(chunk)
            mixed_copy(chunk).start()

        schedule(chunks, reduce, multiply, fetch, sums, finish, ring.event, ring.events, prepare)
        def drain(chunk):
            for item in crossings(chunk):
                item.wait()

        loop(chunks, drain)
        up_spill.start()
        ring.end()
        up_spill.wait()
        ring.settle()
        reduce.end(chunks)
        stats.end(chunks)
        spread.end(chunks)
        for chunk in (chunks - 2, chunks - 1):
            mixed_copy(chunk).wait()
            raw_copy(chunk).wait()

    shape = jax.ShapeDtypeStruct
    out = pl.pallas_call(
        kernel,
        out_shape=[
            shape((length, half), LOW),
            shape((length, width), WIDE),
            shape((2 * chips, length, width), LOW),
            shape((shard * count, hidden), LOW),
            shape((shard * count, hidden), LOW),
            shape((count, inner, down_columns), LOW),
            shape((chips, length, width), LOW),
        ]
        + Reduce.landing(rows, chunks, width, False),
        in_specs=[VMEM, VMEM, VMEM, HBM, HBM, HBM, HBM, HBM],
        out_specs=[HBM] * 8,
        scratch_shapes=[item for group in groups for item in group],
        compiler_params=pltpu.CompilerParams(
            collective_id=collective, has_side_effects=True, vmem_limit_bytes=60 * MIB
        ),
        cost_estimate=pl.CostEstimate(
            flops=2 * length * width * D, bytes_accessed=8 * length * D, transcendentals=0
        ),
    )(attended, weight, gain, tokens, out_grad, gate_shard, up_shard, down_shard)
    return out[:7]


def mlp_forward(
    inputs, gate_full, up_full, down_first, down_second, gain, mixed, upstream, collective
):
    length, inner = inputs.shape[1], gate_full.shape[1]
    width = mixed.shape[1]
    ranks = inputs.shape[0]
    down_columns = down_first.shape[2]
    down_rows = down_first.shape[1]
    chips = lax.axis_size("gx") // 2
    half = chips * width
    chunks = lax.axis_size("gy")
    rows = length // chunks
    tile = min(512, inner)
    pieces = inner // tile

    groups = [
        Reduce.scratch(rows, chunks, width, False),
        Stats.scratch(rows, chunks),
        Spread.scratch(rows, chunks, width),
        [
            pltpu.VMEM((2, rows, half), LOW),
            pltpu.VMEM((rows, width), WIDE),
            pltpu.VMEM((2, rows, width), LOW),
            pltpu.SemaphoreType.DMA((2, chips)),
            pltpu.SemaphoreType.DMA((1,)),
            pltpu.SemaphoreType.DMA((2,)),
        ],
        [
            pltpu.VMEM((D, inner), LOW),
            pltpu.VMEM((D, inner), LOW),
            pltpu.VMEM((inner, D), LOW),
            pltpu.VMEM((2, rows, D), LOW),
            pltpu.VMEM((2, 3, rows, inner), LOW),
            pltpu.SemaphoreType.DMA((pieces, 2)),
            pltpu.SemaphoreType.DMA((2, chunks)),
            pltpu.SemaphoreType.DMA((2, ranks)),
            pltpu.SemaphoreType.DMA((2, 3)),
        ],
    ]

    def kernel(*refs):
        ins, outs, *scratch = take(refs, [8, 7] + [len(g) for g in groups])
        inputs, gate_full, up_full, down_first, down_second, gain, mixed, upstream = ins
        result, grad_out, gain_grad, hidden_out, silu_out, slope_out, cross_land = outs
        gate_weight, up_weight, weight, row_buf, made = scratch[4][:5]
        piece_sems, weight_sem, row_sems, made_sems = scratch[4][5:]
        reduce = Reduce(scratch[0], cross_land, rows, width, False)
        stats = Stats(*scratch[1])
        buffer, local, send, recv = scratch[2]
        spread = Spread(buffer, grad_out, local, send, recv, rows, width)
        up_buf, mixed_buf, result_buf, up_sems, mixed_sems, result_sems = scratch[3]

        def piece_copies(piece):
            at = pl.ds(aligned(piece * tile, tile), tile)
            return [
                pltpu.make_async_copy(gate_full.at[:, at], gate_weight.at[:, at], piece_sems.at[piece, 0]),
                pltpu.make_async_copy(up_full.at[:, at], up_weight.at[:, at], piece_sems.at[piece, 1]),
            ]

        weight_copies = all_blocks(
            down_first, None, down_columns, weight.at[:down_rows], weight_sem.at[0]
        ) + all_blocks(down_second, None, down_columns, weight.at[down_rows:], weight_sem.at[1])

        def row_copy(chunk):
            slot = lax.rem(chunk, 2)
            return all_blocks(
                inputs, row_slice(chunk, rows), width, row_buf.at[slot], row_sems.at[slot]
            )

        def stores(chunk):
            slot, at = lax.rem(chunk, 2), row_slice(chunk, rows)
            return [
                pltpu.make_async_copy(made.at[slot, which], out.at[at], made_sems.at[slot, which])
                for which, out in enumerate((hidden_out, silu_out, slope_out))
            ]

        for item in row_copy(0):
            item.start()
        for piece in range(pieces):
            for item in piece_copies(piece):
                item.start()
        for item in weight_copies:
            item.start()
        greet(True, False)
        gain_grad[...] = jnp.zeros_like(gain_grad)

        def prepare(chunk):
            slot = lax.rem(chunk, 2)
            for item in row_copy(chunk):
                item.wait()

            @pl.when(chunk + 1 < chunks)
            def _():
                for item in row_copy(chunk + 1):
                    item.start()

            @pl.when(chunk >= 2)
            def _():
                for item in stores(chunk - 2):
                    item.wait()

            @pl.loop(0, pieces)
            def _(piece):
                @pl.when(chunk == 0)
                def _():
                    for item in piece_copies(piece):
                        item.wait()

                at = pl.ds(aligned(piece * tile, tile), tile)
                gate = jnp.dot(row_buf[slot], gate_weight[:, at], preferred_element_type=WIDE)
                up = jnp.dot(row_buf[slot], up_weight[:, at], preferred_element_type=WIDE)
                sigma = jax.nn.sigmoid(gate)
                silu = gate * sigma
                made[slot, 0, :, at] = (silu * up).astype(LOW)
                made[slot, 1, :, at] = silu.astype(LOW)
                made[slot, 2, :, at] = (up * (sigma + silu * (1.0 - sigma))).astype(LOW)

            @pl.when(chunk == 0)
            def _():
                for item in weight_copies:
                    item.wait()

            for item in stores(chunk):
                item.start()

        def multiply(chunk, place):
            return jnp.dot(
                made[lax.rem(chunk, 2), 0],
                weight[:, pl.ds(place, width)],
                preferred_element_type=WIDE,
            )

        def up_copy(chunk):
            slot = lax.rem(chunk, 2)
            return all_blocks(
                upstream, row_slice(chunk, rows), width, up_buf.at[slot], up_sems.at[slot]
            )

        def mixed_copy(chunk):
            return pltpu.make_async_copy(
                mixed.at[row_slice(chunk, rows)], mixed_buf, mixed_sems.at[0]
            )

        def result_copy(chunk):
            slot = lax.rem(chunk, 2)
            return pltpu.make_async_copy(
                result_buf.at[slot], result.at[row_slice(chunk, rows)], result_sems.at[slot]
            )

        def fetch(chunk):
            @pl.when(chunk < chunks)
            def _():
                for item in up_copy(chunk):
                    item.start()

            @pl.when(chunk >= 1)
            def _():
                mixed_copy(chunk - 1).start()

        def sums(chunk):
            slot = lax.rem(chunk, 2)
            stats.clear(chunk)
            for item in up_copy(chunk):
                item.wait()

            def tile(at):
                raw = reduce.raw[at]
                up = up_buf[slot, at].astype(WIDE)
                squares = jnp.sum(raw * raw, axis=1, keepdims=True)
                projected = jnp.sum(gain[...] * up * raw, axis=1, keepdims=True)
                stats.put(chunk, at, squares, projected)

            tiles(rows, tile)
            stats.copy(chunk).start()

        def finish(chunk):
            slot = lax.rem(chunk, 2)
            mixed_copy(chunk).wait()
            stats.copy(chunk).wait_recv()
            spread.clear(chunk)

            @pl.when(chunk >= 2)
            def _():
                result_copy(chunk - 2).wait()

            block = pl.ds(aligned(chip_here() * width, width), width)

            def tile(at):
                squares, projected = stats.get(chunk, at)
                factor = lax.rsqrt(squares / D + EPS)
                raw = reduce.raw[at]
                up = up_buf[slot, at].astype(WIDE)
                pull = factor * factor * factor * projected / D
                spread.put(chunk, at, factor * gain[...] * up - raw * pull)
                gain_grad[...] += jnp.sum(up * raw * factor, axis=0, keepdims=True)
                result_buf[slot, at] = (
                    mixed_buf[at] + reduce.raw[at, block] * factor * gain[:, block]
                ).astype(LOW)

            tiles(rows, tile)
            spread.go(chunk)
            result_copy(chunk).start()

        schedule(chunks, reduce, multiply, fetch, sums, finish, prepare=prepare)
        reduce.end(chunks)
        stats.end(chunks)
        spread.end(chunks)
        for chunk in (chunks - 2, chunks - 1):
            result_copy(chunk).wait()
            for item in stores(chunk):
                item.wait()

    shape = jax.ShapeDtypeStruct
    out = pl.pallas_call(
        kernel,
        out_shape=[
            shape((length, width), LOW),
            shape((2 * chips, length, width), LOW),
            shape((1, half), WIDE),
            shape((length, inner), LOW),
            shape((length, inner), LOW),
            shape((length, inner), LOW),
        ]
        + Reduce.landing(rows, chunks, width, False),
        in_specs=[HBM] * 5 + [VMEM, HBM, HBM],
        out_specs=[HBM, HBM, VMEM] + [HBM] * 4,
        scratch_shapes=[item for group in groups for item in group],
        compiler_params=pltpu.CompilerParams(
            collective_id=collective, has_side_effects=True, vmem_limit_bytes=60 * MIB
        ),
        cost_estimate=pl.CostEstimate(
            flops=6 * length * inner * D, bytes_accessed=16 * length * D, transcendentals=0
        ),
    )(inputs, gate_full, up_full, down_first, down_second, gain, mixed, upstream)
    return out[:6]


def mlp_back(gate_grad, up_grad, gate_full, up_full, inputs, gain, upstream, attn_raw, collective):
    length, inner = gate_grad.shape
    half = attn_raw.shape[1]
    chips = lax.axis_size("gx") // 2
    width = half // chips
    count = lax.axis_size("gy")
    chunks = count
    rows = length // chunks
    shard = D // count
    slots, parts = 2, 2

    groups = [
        Reduce.scratch(rows, chunks, width, False),
        Stats.scratch(rows, chunks),
        Spread.scratch(rows, chunks, width),
        RingScatter.scratch(shard, inner, slots, parts),
        [
            pltpu.VMEM((rows, half), LOW),
            pltpu.VMEM((2, rows, half), LOW),
            pltpu.SemaphoreType.DMA((chips,)),
            pltpu.SemaphoreType.DMA((2,)),
            pltpu.SemaphoreType.DMA((1,)),
            pltpu.SemaphoreType.DMA((2,)),
        ],
        Columns.scratch(length, shard),
        [
            pltpu.VMEM((2, length, inner), LOW),
            pltpu.VMEM((2, D, inner), LOW),
            pltpu.SemaphoreType.DMA((2, 2)),
        ],
    ]

    def kernel(*refs):
        ins, outs, *scratch = take(refs, [8, 6] + [len(g) for g in groups])
        gate_grad, up_grad, gate_full, up_full, inputs, gain, upstream, attn_raw = ins
        grads, weights, load_sems = scratch[6]
        grad_copies = [
            pltpu.make_async_copy((gate_grad, up_grad)[way], grads.at[way], load_sems.at[0, way])
            for way in range(2)
        ]
        weight_copies = [
            pltpu.make_async_copy((gate_full, up_full)[way], weights.at[way], load_sems.at[1, way])
            for way in range(2)
        ]
        mixed_out, grad_out, gain_grad, gate_out, up_out, cross_land = outs
        reduce = Reduce(scratch[0], cross_land, rows, width, False)
        stats = Stats(*scratch[1])
        buffer, local, send, recv = scratch[2]
        spread = Spread(buffer, grad_out, local, send, recv, rows, width)
        total, summed, land, ring_send, ring_recv, credit = scratch[3]
        up_buf, raw_buf, up_sems, raw_sems, mixed_sems, out_sems = scratch[4]
        left = Columns(inputs, shard, *scratch[5])

        def product(way, step):
            left.take(ring, way, step)
            tile = 512

            @pl.when(step == 0)
            def _():
                grad_copies[way].wait()

            @pl.loop(0, inner // tile)
            def _(index):
                columns = pl.ds(aligned(index * tile, tile), tile)
                total[way, :, columns] = jnp.dot(
                    left.turned[...], grads[way, :, columns], preferred_element_type=WIDE
                )

        ring = RingScatter(
            product, total, summed, land, ring_send, ring_recv, credit, slots, parts
        )
        left.copy(ring.owner(0, 0)).start()
        for item in grad_copies + weight_copies:
            item.start()
        greet(True, True)
        gain_grad[...] = jnp.zeros_like(gain_grad)

        def prepare(chunk):
            @pl.when(chunk == 0)
            def _():
                for item in weight_copies:
                    item.wait()

        def multiply(chunk, place):
            at = row_slice(chunk, rows)
            return nt(grads[0, at], weights[0, pl.ds(place, width)]) + nt(
                grads[1, at], weights[1, pl.ds(place, width)]
            )

        def up_copy(chunk):
            return all_blocks(upstream, row_slice(chunk, rows), width, up_buf, up_sems)

        def raw_copy(chunk):
            slot = lax.rem(chunk, 2)
            return pltpu.make_async_copy(
                attn_raw.at[row_slice(chunk, rows)], raw_buf.at[slot], raw_sems.at[slot]
            )

        def mixed_copy(chunk):
            return pltpu.make_async_copy(
                reduce.raw.at[:, pl.ds(aligned(chip_here() * width, width), width)],
                mixed_out.at[row_slice(chunk, rows)],
                mixed_sems.at[0],
            )

        def fetch(chunk):
            @pl.when(chunk < chunks)
            def _():
                for item in up_copy(chunk):
                    item.start()
                raw_copy(chunk).start()

        def sums(chunk):
            slot = lax.rem(chunk, 2)
            stats.clear(chunk)
            for item in up_copy(chunk):
                item.wait()
            raw_copy(chunk).wait()

            def tile(at):
                upward = reduce.raw[at] + up_buf[at].astype(WIDE)
                reduce.raw[at] = upward
                raw = raw_buf[slot, at].astype(WIDE)
                squares = jnp.sum(raw * raw, axis=1, keepdims=True)
                projected = jnp.sum(gain[...] * upward * raw, axis=1, keepdims=True)
                stats.put(chunk, at, squares, projected)

            tiles(rows, tile)
            stats.copy(chunk).start()
            mixed_copy(chunk).start()

        def finish(chunk):
            slot = lax.rem(chunk, 2)
            stats.copy(chunk).wait_recv()
            spread.clear(chunk)

            def tile(at):
                squares, projected = stats.get(chunk, at)
                factor = lax.rsqrt(squares / D + EPS)
                upward = reduce.raw[at]
                raw = raw_buf[slot, at].astype(WIDE)
                pull = factor * factor * factor * projected / D
                spread.put(chunk, at, factor * gain[...] * upward - raw * pull)
                gain_grad[...] += jnp.sum(upward * raw * factor, axis=0, keepdims=True)

            tiles(rows, tile)
            spread.go(chunk)
            mixed_copy(chunk).wait()

        schedule(chunks, reduce, multiply, fetch, sums, finish, ring.event, ring.events, prepare)
        writes = [
            pltpu.make_async_copy(total.at[way], (gate_out, up_out)[way], out_sems.at[way])
            for way in range(2)
        ]
        for item in writes:
            item.start()
        ring.end()
        reduce.end(chunks)
        stats.end(chunks)
        spread.end(chunks)
        for item in writes:
            item.wait()

    shape = jax.ShapeDtypeStruct
    out = pl.pallas_call(
        kernel,
        out_shape=[
            shape((length, width), WIDE),
            shape((length, D), LOW),
            shape((1, half), WIDE),
            shape((shard, inner), WIDE),
            shape((shard, inner), WIDE),
        ]
        + Reduce.landing(rows, chunks, width, False),
        in_specs=[HBM, HBM, HBM, HBM, HBM, VMEM, HBM, HBM],
        out_specs=[HBM, HBM, VMEM, HBM, HBM, HBM],
        scratch_shapes=[item for group in groups for item in group],
        compiler_params=pltpu.CompilerParams(
            collective_id=collective, has_side_effects=True, vmem_limit_bytes=60 * MIB
        ),
        cost_estimate=pl.CostEstimate(
            flops=8 * length * inner * D, bytes_accessed=16 * length * D, transcendentals=0
        ),
    )(gate_grad, up_grad, gate_full, up_full, inputs, gain, upstream, attn_raw)
    return out[:5]


class Total:
    def __init__(self, land, send, recv):
        self.land, self.send, self.recv = land, send, recv
        self.count = lax.axis_size("gx")

    @staticmethod
    def scratch(length):
        others = lax.axis_size("gx") - 1
        return [
            pltpu.VMEM((others, 8, length), WIDE),
            pltpu.SemaphoreType.DMA((others,)),
            pltpu.SemaphoreType.DMA((others,)),
        ]

    def copies(self, mine):
        return [
            remote(
                mine,
                self.land.at[shift - 1],
                self.send.at[shift - 1],
                self.recv.at[shift - 1],
                {"gx": rank_at(shift)},
            )
            for shift in range(1, self.count)
        ]

    def start(self, mine):
        for item in self.copies(mine):
            item.start()

    def finish(self, mine):
        for item in self.copies(mine):
            item.wait()
        total = mine[...]
        for shift in range(1, self.count):
            total = total + self.land[shift - 1]
        return total


def gather_in(tokens, stack, output_shard, gains, collective):
    length, width = tokens.shape
    _, shard, side = stack.shape
    columns = 2 * side
    count = lax.axis_size("gy")
    chunks = count
    rows = length // chunks
    chips = lax.axis_size("gx") // 2
    parts = 1
    out_columns = output_shard.shape[1]
    out_rows = width // 2

    groups = [
        RingGather.scratch(parts),
        [
            pltpu.SemaphoreType.DMA((1,)),
            pltpu.SemaphoreType.DMA((2,)),
            pltpu.SemaphoreType.DMA((chips - 1, chunks, 2)),
            pltpu.SemaphoreType.DMA((chips - 1, chunks, 2)),
        ],
        [
            pltpu.VMEM((2, D, side), LOW),
            pltpu.VMEM((2 * chips, length, width), LOW),
            pltpu.VMEM((2, 2, rows, width), WIDE),
            pltpu.VMEM((2, rows, width), LOW),
            pltpu.VMEM((length, STATS), WIDE),
            pltpu.VMEM((8, length), WIDE),
            pltpu.SemaphoreType.DMA((2,)),
            pltpu.SemaphoreType.DMA((2, 3)),
        ],
        Total.scratch(length),
        [
            pltpu.VMEM((chips - 1, 8, width), WIDE),
            pltpu.SemaphoreType.DMA((chips - 1, 2)),
        ],
        RingGather.scratch(1),
        [pltpu.VMEM((count, width, out_columns), LOW)],
    ]

    def kernel(*refs):
        ins, outs, *scratch = take(refs, [4, 8] + [len(g) for g in groups])
        tokens, stack, output_shard, gains = ins
        whole, full, output_full, query_raw, key_raw, values, squares, halves = outs
        out_held = scratch[6][0]
        gain_land, gain_sems = scratch[4]
        own_sem, core_sems, cross_sems, pass_sems = scratch[1]
        weight, held, raw_buf, value_buf, stats, mine = scratch[2][:6]
        copy_sems, out_sems = scratch[2][6:]
        total = Total(*scratch[3])

        def slot(way, owner, part):
            return weight.at[way, pl.ds(aligned(owner * shard, shard), shard)]

        def spill(way, owner, part):
            return full.at[way, pl.ds(aligned(owner * shard, shard), shard)]

        def source(way, part):
            return stack.at[way]

        ring = RingGather(source, slot, spill, parts, *scratch[0])

        def out_slot(way, owner, part):
            return out_held.at[owner, way * out_rows : (way + 1) * out_rows]

        def out_spill(way, owner, part):
            at = pl.ds(aligned(owner * out_columns, out_columns), out_columns)
            return output_full.at[way * out_rows : (way + 1) * out_rows, at]

        def out_source(way, part):
            return output_shard.at[way * out_rows : (way + 1) * out_rows]

        out_ring = RingGather(out_source, out_slot, out_spill, 1, *scratch[5])

        def block(rank, chunk):
            if chunk is None:
                return held.at[rank]
            return held.at[rank, row_slice(chunk, rows)]

        here = lax.axis_index("gx")
        own = pltpu.make_async_copy(tokens, block(here, None), own_sem.at[0])
        core = remote(
            block(here, None), block(here, None), core_sems.at[0], core_sems.at[1], {"gx": other_core()}
        )

        def cross(shift, chunk):
            return remote(
                block(here, chunk),
                block(here, chunk),
                cross_sems.at[shift - 1, chunk, 0],
                cross_sems.at[shift - 1, chunk, 1],
                {"gx": peer_at(shift)},
            )

        def onward(shift, chunk):
            spot = block(peer_at(chips - shift), chunk)
            return remote(
                spot,
                spot,
                pass_sems.at[shift - 1, chunk, 0],
                pass_sems.at[shift - 1, chunk, 1],
                {"gx": other_core()},
            )

        gain_copies = [
            remote(
                gains,
                gain_land.at[shift - 1],
                gain_sems.at[shift - 1, 0],
                gain_sems.at[shift - 1, 1],
                {"gx": peer_at(shift)},
            )
            for shift in range(1, chips)
        ]
        own.start()
        greet("all", True)
        for item in gain_copies:
            item.start()
        ring.begin()
        own.wait()

        def send(chunk):
            for shift in range(1, chips):
                cross(shift, chunk).start()

        loop(chunks, send)
        core.start()

        def step(chunk):
            for shift in range(1, chips):
                cross(shift, chunk).wait_recv()
                onward(shift, chunk).start()

            @pl.when(chunk < ring.events)
            def _():
                ring.event(chunk)

        loop(chunks, step)
        out_ring.begin()
        ring.end()

        def drain(chunk):
            for shift in range(1, chips):
                cross(shift, chunk).wait_send()
                onward(shift, chunk).wait()

        loop(chunks, drain)
        core.wait()
        whole_copy = pltpu.make_async_copy(held, whole, copy_sems.at[0])
        whole_copy.start()

        def stores(chunk):
            slot, at = lax.rem(chunk, 2), row_slice(chunk, rows)
            return [
                pltpu.make_async_copy(raw_buf.at[slot, 0], query_raw.at[at], out_sems.at[slot, 0]),
                pltpu.make_async_copy(raw_buf.at[slot, 1], key_raw.at[at], out_sems.at[slot, 1]),
                pltpu.make_async_copy(value_buf.at[slot], values.at[at], out_sems.at[slot, 2]),
            ]

        lane = lax.broadcasted_iota(jnp.int32, (rows, STATS), 1)

        def project(chunk):
            slot = lax.rem(chunk, 2)
            @pl.when(chunk >= 2)
            def _():
                for item in stores(chunk - 2):
                    item.wait()

            at = row_slice(chunk, rows)
            middle = side - width

            def against(way, columns):
                raw = jnp.zeros((rows, columns.stop - columns.start), WIDE)
                for rank in range(2 * chips):
                    raw = raw + jnp.dot(
                        held[rank, at],
                        weight[way, rank * width : (rank + 1) * width, columns],
                        preferred_element_type=WIDE,
                    )
                return raw

            some = []
            raw_buf[slot, 0] = against(0, slice(0, width))
            raw_buf[slot, 1, :, :middle] = against(0, slice(width, side))
            raw_buf[slot, 1, :, middle:] = against(1, slice(0, middle))
            value_buf[slot] = against(1, slice(middle, side)).astype(LOW)
            for which in range(2):
                raw = raw_buf[slot, which]
                some.append(jnp.sum(raw * raw, axis=1, keepdims=True))
            stats[row_slice(chunk, rows)] = jnp.where(lane == 0, some[0], some[1])
            for item in stores(chunk):
                item.start()

            @pl.when(chunk < out_ring.events)
            def _():
                out_ring.event(chunk)

        loop(chunks, project)
        mine[...] = stats[...].T[:8]
        total.start(mine)
        for chunk in (chunks - 2, chunks - 1):
            for item in stores(chunk):
                item.wait()
        squares[...] = total.finish(mine)
        whole_copy.wait()
        ring.settle()
        out_ring.end()
        out_ring.settle()
        halves[:, pl.ds(aligned(chip_here() * width, width), width)] = gains[...]
        for shift in range(1, chips):
            gain_copies[shift - 1].wait()
            chip = lax.rem(chip_here() + chips - shift, chips)
            halves[:, pl.ds(aligned(chip * width, width), width)] = gain_land[shift - 1]

    shape = jax.ShapeDtypeStruct
    return pl.pallas_call(
        kernel,
        out_shape=[
            shape((2 * chips, length, width), LOW),
            shape((2, shard * count, side), LOW),
            shape((width, D), LOW),
            shape((length, width), WIDE),
            shape((length, width), WIDE),
            shape((length, width), LOW),
            shape((8, length), WIDE),
            shape((8, chips * width), WIDE),
        ],
        in_specs=[HBM, HBM, HBM, VMEM],
        out_specs=[HBM] * 6 + [VMEM, VMEM],
        scratch_shapes=[item for group in groups for item in group],
        compiler_params=pltpu.CompilerParams(
            collective_id=collective, has_side_effects=True, vmem_limit_bytes=40 * MIB
        ),
        cost_estimate=pl.CostEstimate(
            flops=2 * length * columns * D, bytes_accessed=8 * length * D, transcendentals=0
        ),
    )(tokens, stack, output_shard, gains)


def hidden_back(blocks, down_first, down_second, hidden, silu, slope, collective):
    length, inner = hidden.shape
    count = lax.axis_size("gy")
    chunks = count
    rows = length // chunks
    shard = D // count
    side = inner // 2
    slots, parts = 3, 2
    down_rows = down_first.shape[1]
    tile = min(512, inner)

    groups = [
        RingScatter.scratch(shard, side, slots, parts),
        [
            pltpu.VMEM((2, 2, rows, inner), LOW),
            pltpu.VMEM((2, 2, rows, inner), LOW),
            pltpu.SemaphoreType.DMA((2, 2)),
            pltpu.SemaphoreType.DMA((2, 2)),
            pltpu.SemaphoreType.DMA((2,)),
            pltpu.VMEM((count, shard, length), LOW),
        ],
        [
            pltpu.VMEM((length, D), LOW),
            pltpu.VMEM((inner, D), LOW),
            pltpu.SemaphoreType.DMA((blocks.shape[0],)),
            pltpu.SemaphoreType.DMA((2, count)),
        ],
    ]

    def kernel(*refs):
        ins, outs, *scratch = take(refs, [6, 3] + [len(g) for g in groups])
        blocks, down_first, down_second, hidden, silu, slope = ins
        grad, weight, grad_sems, weight_sems = scratch[2]
        gate_grad, up_grad, weight_grad = outs
        total, summed, land, ring_send, ring_recv, credit = scratch[0]
        given, made, given_sems, made_sems, out_sems, turned = scratch[1]

        def product(way, step):
            owner = ring.owner(way, step)

            @pl.when((step < count // 2) | (step == count - 1))
            def _():
                turned[owner] = grad[:, pl.ds(aligned(owner * shard, shard), shard)].T

            size = min(512, side)

            @pl.loop(0, side // size)
            def _(index):
                at = pl.ds(aligned(index * size, size), size)
                take_at = pl.ds(aligned(way * side + index * size, size), size)
                total[way, :, at] = jnp.dot(
                    turned[owner], hidden[:, take_at], preferred_element_type=WIDE
                )

        ring = RingScatter(
            product, total, summed, land, ring_send, ring_recv, credit, slots, parts
        )

        def load(chunk):
            slot = lax.rem(chunk, 2)
            return [
                pltpu.make_async_copy(
                    (slope, silu)[which].at[row_slice(chunk, rows)],
                    given.at[slot, which],
                    given_sems.at[slot, which],
                )
                for which in range(2)
            ]

        def store(chunk):
            slot = lax.rem(chunk, 2)
            return [
                pltpu.make_async_copy(
                    made.at[slot, which],
                    (gate_grad, up_grad)[which].at[row_slice(chunk, rows)],
                    made_sems.at[slot, which],
                )
                for which in range(2)
            ]

        grad_copies = all_blocks(blocks, None, blocks.shape[2], grad, grad_sems)
        weight_copies = all_blocks(
            down_first, None, shard, weight.at[:down_rows], weight_sems.at[0]
        ) + all_blocks(down_second, None, shard, weight.at[down_rows:], weight_sems.at[1])
        for item in grad_copies + weight_copies + load(0):
            item.start()
        greet(False, True)
        for item in grad_copies:
            item.wait()

        def iteration(step):
            slot = lax.rem(step, 2)
            for part in range(parts):
                ring.event(step * parts + part)

            @pl.when(step + 1 < chunks)
            def _():
                for item in load(step + 1):
                    item.start()

            @pl.when(step >= 2)
            def _():
                for item in store(step - 2):
                    item.wait()

            for item in load(step):
                item.wait()

            @pl.when(step == 0)
            def _():
                for item in weight_copies:
                    item.wait()

            @pl.loop(0, inner // tile)
            def _(index):
                at = pl.ds(aligned(index * tile, tile), tile)
                hidden_grad = lax.dot_general(
                    grad[row_slice(step, rows)],
                    weight[at],
                    (((1,), (1,)), ((), ())),
                    preferred_element_type=WIDE,
                )
                for which in range(2):
                    made[slot, which, :, at] = (
                        hidden_grad * given[slot, which, :, at].astype(WIDE)
                    ).astype(LOW)

            for item in store(step):
                item.start()

        loop(chunks, iteration)
        writes = [
            pltpu.make_async_copy(
                total.at[way], weight_grad.at[:, way * side : (way + 1) * side], out_sems.at[way]
            )
            for way in range(2)
        ]
        for item in writes:
            item.start()
        for chunk in (chunks - 2, chunks - 1):
            for item in store(chunk):
                item.wait()
        ring.end()
        for item in writes:
            item.wait()

    shape = jax.ShapeDtypeStruct
    return pl.pallas_call(
        kernel,
        out_shape=[
            shape((length, inner), LOW),
            shape((length, inner), LOW),
            shape((shard, inner), WIDE),
        ],
        in_specs=[HBM, HBM, HBM, VMEM, HBM, HBM],
        out_specs=[HBM, HBM, HBM],
        scratch_shapes=[item for group in groups for item in group],
        compiler_params=pltpu.CompilerParams(
            collective_id=collective, has_side_effects=True, vmem_limit_bytes=60 * MIB
        ),
        cost_estimate=pl.CostEstimate(
            flops=4 * length * inner * D, bytes_accessed=16 * length * D, transcendentals=0
        ),
    )(blocks, down_first, down_second, hidden, silu, slope)


def attn_in_back(
    query_back,
    key_back,
    value_grad,
    query_raw,
    key_raw,
    factors,
    projections,
    query_gain,
    key_gain,
    stack,
    inputs,
    mixed_grad,
    gain_parts,
    collective,
):
    length, columns = value_grad.shape[0], 2 * stack.shape[2]
    width = mixed_grad.shape[1]
    count = lax.axis_size("gy")
    chunks = count
    rows = length // chunks
    shard = D // count
    side = columns // 2
    slots, parts = count - 1, 2
    tile = 256 if side % 256 == 0 else 128

    groups = [
        Reduce.scratch(rows, chunks, width, True),
        RingScatter.scratch(shard, side, slots, parts),
        [
            pltpu.VMEM((rows, width), WIDE),
            pltpu.VMEM((2, rows, width), WIDE),
            pltpu.VMEM((length, columns), LOW),
            pltpu.VMEM((length, STATS), WIDE),
            pltpu.VMEM((2, 4, rows, width), WIDE),
            pltpu.VMEM((2, D, side), LOW),
            pltpu.SemaphoreType.DMA((2, 4)),
            pltpu.SemaphoreType.DMA((2,)),
            pltpu.SemaphoreType.DMA((1,)),
            pltpu.SemaphoreType.DMA((2,)),
            pltpu.SemaphoreType.DMA((2,)),
        ],
        Columns.scratch(length, shard),
        Total.scratch(length),
        [
            pltpu.VMEM((8, width), WIDE),
            pltpu.VMEM((count - 1, 8, width), WIDE),
            pltpu.SemaphoreType.DMA((count - 1, 2)),
        ],
    ]

    def kernel(*refs):
        ins, outs, *scratch = take(refs, [16, 4] + [len(g) for g in groups])
        query_back, key_back, value_grad, query_raw, key_raw, factors = ins[:6]
        projections, query_gain, key_gain, full, inputs, mixed_grad = ins[6:12]
        gain_parts = ins[12:]
        token_grad, weight_grad, gain_grads, cross_land = outs
        gain_mine, gain_land, gain_sems = scratch[5]
        reduce = Reduce(scratch[0], cross_land, rows, width, True)
        total, summed, land, ring_send, ring_recv, credit = scratch[1]
        mixed_buf, token_buf, grads, projected, given, stack = scratch[2][:6]
        given_sems, whole_sems, mixed_sems, token_sems, out_sems = scratch[2][6:]
        left = Columns(inputs, shard, *scratch[3])
        total_sum = Total(*scratch[4])

        def product(way, step):
            left.take(ring, way, step)

            @pl.loop(0, side // tile)
            def _(index):
                at = pl.ds(aligned(index * tile, tile), tile)
                take_at = pl.ds(aligned(way * side + index * tile, tile), tile)
                total[way, :, at] = jnp.dot(
                    left.turned[...], grads[:, take_at], preferred_element_type=WIDE
                )

        ring = RingScatter(
            product, total, summed, land, ring_send, ring_recv, credit, slots, parts
        )
        def load(chunk):
            slot, at = lax.rem(chunk, 2), row_slice(chunk, rows)
            return [
                pltpu.make_async_copy(
                    source.at[at], given.at[slot, which], given_sems.at[slot, which]
                )
                for which, source in enumerate((query_back, key_back, query_raw, key_raw))
            ]

        value_copy = pltpu.make_async_copy(value_grad, grads.at[:, 2 * width :], whole_sems.at[0])
        stack_copy = pltpu.make_async_copy(full, stack, whole_sems.at[1])
        left.copy(ring.owner(0, 0)).start()
        for item in load(0):
            item.start()
        value_copy.start()
        stack_copy.start()
        chip_columns = pl.ds(aligned(chip_here() * width, width), width)
        gain_mine[...] = jnp.zeros_like(gain_mine)
        for which, part in enumerate(gain_parts):
            gain_mine[which : which + 1] = part[...] if which < 2 else part[:, chip_columns]
        greet("all", False, True)
        total_sum.start(projections)
        gain_copies = [
            remote(
                gain_mine,
                gain_land.at[shift - 1],
                gain_sems.at[shift - 1, 0],
                gain_sems.at[shift - 1, 1],
                {"gy": block_at(shift)},
            )
            for shift in range(1, count)
        ]
        for item in gain_copies:
            item.start()
        sums_here = total_sum.finish(projections)
        projected[...] = jnp.concatenate([sums_here] * (STATS // 8), axis=0).T

        def form(chunk):
            slot = lax.rem(chunk, 2)

            @pl.when(chunk + 1 < chunks)
            def _():
                for item in load(chunk + 1):
                    item.start()

            for item in load(chunk):
                item.wait()

            def some(part):
                at = pl.ds(aligned(chunk * rows + part.start, 32), 32)
                for which, gain in enumerate((query_gain, key_gain)):
                    factor = factors[at, which : which + 1]
                    pull = factor * factor * factor * projected[at, which : which + 1] / D
                    back, raw = given[slot, which, part], given[slot, which + 2, part]
                    grads[at, which * width : (which + 1) * width] = (
                        factor * gain[...] * back - raw * pull
                    ).astype(LOW)

            tiles(rows, some)

        loop(chunks, form)
        value_copy.wait()

        def prepare(chunk):
            @pl.when(chunk == 0)
            def _():
                stack_copy.wait()

        def multiply(chunk, place):
            at = row_slice(chunk, rows)
            return nt(grads[at, :side], stack[0, pl.ds(place, width)]) + nt(
                grads[at, side:], stack[1, pl.ds(place, width)]
            )

        def mixed_copy(chunk):
            return pltpu.make_async_copy(
                mixed_grad.at[row_slice(chunk, rows)], mixed_buf, mixed_sems.at[0]
            )

        def token_copy(chunk):
            slot = lax.rem(chunk, 2)
            return pltpu.make_async_copy(
                token_buf.at[slot], token_grad.at[row_slice(chunk, rows)], token_sems.at[slot]
            )

        def fetch(chunk):
            @pl.when(chunk >= 1)
            def _():
                mixed_copy(chunk - 1).start()

        def sums(chunk):
            pass

        def finish(chunk):
            slot = lax.rem(chunk, 2)
            mixed_copy(chunk).wait()

            @pl.when(chunk >= 2)
            def _():
                token_copy(chunk - 2).wait()

            def some(at):
                token_buf[slot, at] = mixed_buf[at] + reduce.raw[at]

            tiles(rows, some)
            token_copy(chunk).start()

        schedule(chunks, reduce, multiply, fetch, sums, finish, ring.event, ring.events, prepare)
        writes = [
            pltpu.make_async_copy(
                total.at[way], weight_grad.at[:, way * side : (way + 1) * side], out_sems.at[way]
            )
            for way in range(2)
        ]
        for item in writes:
            item.start()
        gain_total = gain_mine[...]
        for shift in range(1, count):
            gain_copies[shift - 1].wait()
            gain_total = gain_total + gain_land[shift - 1]
        gain_grads[...] = gain_total
        ring.end()
        reduce.end(chunks)
        for chunk in (chunks - 2, chunks - 1):
            token_copy(chunk).wait()
        for item in writes:
            item.wait()

    shape = jax.ShapeDtypeStruct
    out = pl.pallas_call(
        kernel,
        out_shape=[
            shape((length, width), WIDE),
            shape((shard, columns), WIDE),
            shape((8, width), WIDE),
        ]
        + Reduce.landing(rows, chunks, width, True),
        in_specs=[HBM] * 5 + [VMEM] * 4 + [HBM] * 3 + [VMEM] * 4,
        out_specs=[HBM, HBM, VMEM, HBM],
        scratch_shapes=[item for group in groups for item in group],
        compiler_params=pltpu.CompilerParams(
            collective_id=collective, has_side_effects=True, vmem_limit_bytes=60 * MIB
        ),
        cost_estimate=pl.CostEstimate(
            flops=4 * length * columns * D, bytes_accessed=8 * length * D, transcendentals=0
        ),
    )(
        query_back,
        key_back,
        value_grad,
        query_raw,
        key_raw,
        factors,
        projections,
        query_gain,
        key_gain,
        stack,
        inputs,
        mixed_grad,
        *gain_parts,
    )
    return out[:3]


def token_positions(segment):
    length = segment.shape[0]
    labels = jnp.arange(SEGS, dtype=jnp.int32)
    member = (segment[:, None] == labels[None, :]).astype(jnp.int32)
    totals = jnp.sum(member, axis=0)
    starts = jnp.cumsum(totals) - totals
    opening = jnp.sum(member * starts[None, :], axis=1)
    return jnp.arange(length, dtype=jnp.int32) - opening


def rotary_tables(segment):
    place = token_positions(segment).astype(jnp.float32)
    halves = HEAD // 2
    inverse = jnp.exp(jnp.arange(halves, dtype=jnp.float32) * (-2.0 * math.log(THETA) / HEAD))
    angle = place[:, None] * inverse[None, :]
    return (jnp.cos(angle), jnp.sin(angle))


BLOCK = 256
LANES = 128
SCALE = 1.0 / math.sqrt(HEAD)
SCALE_TWO = SCALE * math.log2(math.e)


def turn(values, cosine, sine):
    return values * cosine + pltpu.roll(values, HEAD // 2, 1) * sine


def head_columns(head):
    return slice(head * HEAD, (head + 1) * HEAD)


def nt(left, right):
    return lax.dot_general(left, right, (((1,), (1,)), ((), ())), preferred_element_type=WIDE)


def attend(first_block, query_raw, key_raw, values, factors, query_gain, key_gain, tables, starts):
    length, width = query_raw.shape
    heads = width // HEAD

    def kernel(
        first_block,
        query_raw,
        key_raw,
        values,
        factors,
        query_gain,
        key_gain,
        cosine,
        sine,
        starts,
        queries,
        keys,
        attended,
        peaks,
        peak_columns,
        given,
        held_values,
        given_sems,
        value_sem,
    ):
        def load(index):
            slot, at = lax.rem(index, 2), row_slice(index, BLOCK)
            return [
                pltpu.make_async_copy(
                    source.at[at], given.at[slot, which], given_sems.at[slot, which]
                )
                for which, source in enumerate((query_raw, key_raw))
            ]

        value_copy = pltpu.make_async_copy(values, held_values, value_sem.at[0])
        for item in load(0):
            item.start()
        value_copy.start()

        def norm_block(index):
            at = row_slice(index, BLOCK)
            slot = lax.rem(index, 2)

            @pl.when(index + 1 < length // BLOCK)
            def _():
                for item in load(index + 1):
                    item.start()

            for item in load(index):
                item.wait()
            cos, sin = cosine[at], sine[at]
            for which, (gain, out) in enumerate(((query_gain, queries), (key_gain, keys))):
                factor = factors[at, which : which + 1]
                for head in range(heads):
                    columns = head_columns(head)
                    normed = given[slot, which, :, columns] * factor * gain[:, columns]
                    out[at, columns] = turn(normed, cos, sin).astype(LOW)

        loop(length // BLOCK, norm_block)
        value_copy.wait()

        lane = lax.broadcasted_iota(jnp.int32, (BLOCK, LANES), 1)
        row_index = lax.broadcasted_iota(jnp.int32, (BLOCK, BLOCK), 0)
        column_index = lax.broadcasted_iota(jnp.int32, (BLOCK, BLOCK), 1)

        def query_block(index):
            at = row_slice(index, BLOCK)
            start = starts[at]

            def key_block(other, carry):
                there = row_slice(other, BLOCK)
                key_place = column_index + other * BLOCK
                allowed = (key_place >= start) & (key_place <= row_index + index * BLOCK)
                made = []
                for head in range(heads):
                    columns = head_columns(head)
                    peak, total, rows = carry[head]
                    scores = nt(queries[at, columns], keys[there, columns]) * SCALE_TWO
                    scores = jnp.where(allowed, scores, NEGATIVE)
                    higher = jnp.maximum(peak, jnp.max(scores, axis=1, keepdims=True))
                    raised = jnp.exp2(scores - higher)
                    shrink = jnp.exp2(peak - higher)
                    total = total * shrink + jnp.sum(raised, axis=1, keepdims=True)
                    rows = rows * shrink + jnp.dot(
                        raised.astype(LOW), held_values[there, columns], preferred_element_type=WIDE
                    )
                    made.append((higher, total, rows))
                return tuple(made)

            empty = (
                jnp.full((BLOCK, 1), NEGATIVE, WIDE),
                jnp.zeros((BLOCK, 1), WIDE),
                jnp.zeros((BLOCK, HEAD), WIDE),
            )
            done = lax.fori_loop(first_block[index], index + 1, key_block, (empty,) * heads)
            column = jnp.zeros((BLOCK, LANES), WIDE)
            for head in range(heads):
                peak, total, rows = done[head]
                attended[at, head_columns(head)] = (rows / total).astype(LOW)
                column = jnp.where(lane == head, peak + jnp.log2(total), column)
            peak_columns[at] = column

        loop(length // BLOCK, query_block)
        peaks[...] = peak_columns[...].T[:8]

    shape = jax.ShapeDtypeStruct
    smem = pl.BlockSpec(memory_space=pltpu.SMEM)
    return pl.pallas_call(
        kernel,
        out_shape=[
            shape((length, width), LOW),
            shape((length, width), LOW),
            shape((length, width), LOW),
            shape((8, length), WIDE),
        ],
        in_specs=[smem] + [HBM] * 3 + [VMEM] * 6,
        out_specs=[VMEM] * 4,
        scratch_shapes=[
            pltpu.VMEM((length, LANES), WIDE),
            pltpu.VMEM((2, 2, BLOCK, width), WIDE),
            pltpu.VMEM((length, width), LOW),
            pltpu.SemaphoreType.DMA((2, 2)),
            pltpu.SemaphoreType.DMA((1,)),
        ],
        compiler_params=pltpu.CompilerParams(vmem_limit_bytes=48 * MIB),
        cost_estimate=pl.CostEstimate(
            flops=2 * length * MAX_LEN * width,
            bytes_accessed=16 * length * width,
            transcendentals=length * MAX_LEN * heads // 2,
        ),
    )(first_block, query_raw, key_raw, values, factors, query_gain, key_gain, *tables, starts)


def attend_back(
    last_block,
    queries,
    keys,
    values,
    attended,
    upstream,
    peaks,
    query_raw,
    key_raw,
    factors,
    query_gain,
    key_gain,
    tables,
    start_row,
):
    length, width = query_raw.shape
    heads = width // HEAD

    def kernel(
        last_block,
        queries,
        keys,
        values,
        attended,
        upstream,
        peaks,
        query_raw,
        key_raw,
        factors,
        query_gain,
        key_gain,
        cosine,
        sine,
        start_row,
        query_out,
        key_out,
        value_out,
        projections,
        query_gain_grad,
        key_gain_grad,
        query_sum,
        key_sum,
        value_sum,
        columns_scratch,
        deltas,
        held_query,
        held_key,
        made,
        load_sems,
        made_sems,
    ):
        loads = [
            pltpu.make_async_copy(query_raw, held_query, load_sems.at[0]),
            pltpu.make_async_copy(key_raw, held_key, load_sems.at[1]),
        ]
        for item in loads:
            item.start()

        def store(index, out):
            slot = lax.rem(index, 2)
            return pltpu.make_async_copy(
                made.at[slot], out.at[row_slice(index, BLOCK)], made_sems.at[slot]
            )

        lane = lax.broadcasted_iota(jnp.int32, (BLOCK, LANES), 1)
        query_gain_grad[...] = jnp.zeros_like(query_gain_grad)
        key_gain_grad[...] = jnp.zeros_like(key_gain_grad)

        def prepare(index):
            at = row_slice(index, BLOCK)
            column = jnp.zeros((BLOCK, LANES), WIDE)
            for head in range(heads):
                columns = head_columns(head)
                delta = jnp.sum(
                    attended[at, columns].astype(WIDE) * upstream[at, columns].astype(WIDE),
                    axis=1,
                    keepdims=True,
                )
                column = jnp.where(lane == head, delta, column)
            columns_scratch[at] = column
            query_sum[at] = jnp.zeros((BLOCK, width), WIDE)

        loop(length // BLOCK, prepare)
        deltas[...] = columns_scratch[...].T[:8]
        row_index = lax.broadcasted_iota(jnp.int32, (BLOCK, BLOCK), 0)
        column_index = lax.broadcasted_iota(jnp.int32, (BLOCK, BLOCK), 1)

        def turn_back(index, summed, raw, gain, factor, out, gain_grad):
            at, slot = row_slice(index, BLOCK), lax.rem(index, 2)

            @pl.when(index >= 2)
            def _():
                store(index - 2, out).wait()

            cos, sin = cosine[at], sine[at]
            share = jnp.zeros((BLOCK, 1), WIDE)
            for head in range(heads):
                columns = head_columns(head)
                normed = turn(summed(head) * SCALE, cos, -sin)
                made[slot, :, columns] = normed
                weighed = normed * raw[at, columns]
                share += jnp.sum(gain[:, columns] * weighed, axis=1, keepdims=True)
                gain_grad[:, columns] += jnp.sum(weighed * factor, axis=0, keepdims=True)
            store(index, out).start()
            return share

        def key_block(index):
            at = row_slice(index, BLOCK)
            key_sum[...] = jnp.zeros_like(key_sum)
            value_sum[...] = jnp.zeros_like(value_sum)

            def query_block(other, carry):
                there = row_slice(other, BLOCK)
                key_place = row_index + index * BLOCK
                allowed = (key_place >= start_row[:, there]) & (
                    key_place <= column_index + other * BLOCK
                )
                for head in range(heads):
                    columns = head_columns(head)
                    scores = nt(keys[at, columns], queries[there, columns]) * SCALE_TWO
                    scores = jnp.where(allowed, scores, NEGATIVE)
                    chance = jnp.exp2(scores - peaks[head : head + 1, there])
                    value_sum[:, columns] += jnp.dot(
                        chance.astype(LOW), upstream[there, columns], preferred_element_type=WIDE
                    )
                    chance_grad = nt(values[at, columns], upstream[there, columns])
                    score_grad = (chance * (chance_grad - deltas[head : head + 1, there])).astype(LOW)
                    key_sum[:, columns] += jnp.dot(
                        score_grad, queries[there, columns], preferred_element_type=WIDE
                    )
                    query_sum[there, columns] += lax.dot_general(
                        score_grad,
                        keys[at, columns],
                        (((0,), (0,)), ((), ())),
                        preferred_element_type=WIDE,
                    )
                return carry

            lax.fori_loop(index, last_block[index] + 1, query_block, 0)
            value_out[at] = value_sum[...].astype(LOW)

            @pl.when(index == 0)
            def _():
                loads[1].wait()

            share = turn_back(
                index,
                lambda head: key_sum[:, head_columns(head)],
                held_key,
                key_gain,
                factors[at, 1:2],
                key_out,
                key_gain_grad,
            )
            columns_scratch[at] = jnp.where(lane == 1, share, 0.0)

        loop(length // BLOCK, key_block)
        for index in (length // BLOCK - 2, length // BLOCK - 1):
            store(index, key_out).wait()
        loads[0].wait()

        def finish(index):
            at = row_slice(index, BLOCK)
            share = turn_back(
                index,
                lambda head: query_sum[at, head_columns(head)],
                held_query,
                query_gain,
                factors[at, 0:1],
                query_out,
                query_gain_grad,
            )
            columns_scratch[at] += jnp.where(lane == 0, share, 0.0)

        loop(length // BLOCK, finish)
        for index in (length // BLOCK - 2, length // BLOCK - 1):
            store(index, query_out).wait()
        projections[...] = columns_scratch[...].T[:8]

    shape = jax.ShapeDtypeStruct
    smem = pl.BlockSpec(memory_space=pltpu.SMEM)
    return pl.pallas_call(
        kernel,
        out_shape=[
            shape((length, width), WIDE),
            shape((length, width), WIDE),
            shape((length, width), LOW),
            shape((8, length), WIDE),
            shape((1, width), WIDE),
            shape((1, width), WIDE),
        ],
        in_specs=[smem] + [VMEM] * 6 + [HBM] * 2 + [VMEM] * 6,
        out_specs=[HBM] * 2 + [VMEM] * 4,
        scratch_shapes=[
            pltpu.VMEM((length, width), WIDE),
            pltpu.VMEM((BLOCK, width), WIDE),
            pltpu.VMEM((BLOCK, width), WIDE),
            pltpu.VMEM((length, LANES), WIDE),
            pltpu.VMEM((8, length), WIDE),
            pltpu.VMEM((length, width), WIDE),
            pltpu.VMEM((length, width), WIDE),
            pltpu.VMEM((2, BLOCK, width), WIDE),
            pltpu.SemaphoreType.DMA((2,)),
            pltpu.SemaphoreType.DMA((2,)),
        ],
        compiler_params=pltpu.CompilerParams(vmem_limit_bytes=52 * MIB),
        cost_estimate=pl.CostEstimate(
            flops=5 * length * MAX_LEN * width,
            bytes_accessed=32 * length * width,
            transcendentals=length * MAX_LEN * heads // 2,
        ),
    )(
        last_block,
        queries,
        keys,
        values,
        attended,
        upstream,
        peaks,
        query_raw,
        key_raw,
        factors,
        query_gain,
        key_gain,
        *tables,
        start_row,
    )


def shards(
    tokens,
    query_weight,
    key_weight,
    value_weight,
    output_weight,
    gate_weight,
    up_weight,
    down_weight,
    query_gain,
    key_gain,
    attn_gain,
    mlp_gain,
    seq_ids,
    out_grad,
):
    segment = seq_ids[0]
    length = tokens.shape[0]
    local_width = tokens.shape[1]
    cosine, sine = rotary_tables(segment)
    tables = (
        jnp.concatenate([cosine, cosine], axis=1),
        jnp.concatenate([-sine, sine], axis=1),
    )
    order = jnp.arange(length, dtype=jnp.int32)
    starts = order - token_positions(segment)
    blocks = length // BLOCK
    first_block = starts.reshape(blocks, BLOCK)[:, 0] // BLOCK
    closing = segment.reshape(blocks, BLOCK)[:, -1]
    ends = jnp.sum((segment[None, :] <= closing[:, None]).astype(jnp.int32), axis=1) - 1
    last_block = ends // BLOCK
    gains = jnp.concatenate([attn_gain[None], mlp_gain[None], jnp.zeros((6, local_width))], axis=0)
    query_gain, key_gain = query_gain.reshape(1, -1), key_gain.reshape(1, -1)
    middle = local_width // 2
    pairs = (
        (query_weight, key_weight[:, :middle]),
        (key_weight[:, middle:], value_weight),
    )
    stack = jnp.stack([jnp.concatenate(pair, axis=1) for pair in pairs])
    inputs, attn_stack, output_full, query_raw, key_raw, values, squares, halves = gather_in(
        tokens, stack, output_weight, gains, 1
    )
    attn_half, mlp_half = halves[:1], halves[1:2]
    middle = down_weight.shape[0] // 2
    squares, down_rows = lax.optimization_barrier((squares, down_weight[middle:]))
    down_second = lax.all_gather(down_rows, "gy", axis=0)
    factors = lax.rsqrt(squares[:2].T / D + EPS)
    queries, keys, attended, peaks = attend(
        first_block,
        query_raw,
        key_raw,
        values,
        factors,
        query_gain,
        key_gain,
        tables,
        starts[:, None],
    )
    attn_raw, mixed, mlp_inputs, gate_full, up_full, down_first, upstream = attn_out(
        attended, output_full, attn_half, inputs, out_grad, gate_weight, up_weight, down_weight[:middle], 2
    )
    result, mlp_full, mlp_gain_part, hidden, silu, slope = mlp_forward(
        mlp_inputs, gate_full, up_full, down_first, down_second, mlp_half, mixed, upstream, 3
    )
    gate_grad, up_grad, down_turned = hidden_back(
        mlp_full, down_first, down_second, hidden, silu, slope, 4
    )
    down_weight_grad = down_turned.T
    mixed_grad, attn_full, attn_gain_part, gate_weight_grad, up_weight_grad = mlp_back(
        gate_grad, up_grad, gate_full, up_full, mlp_inputs, attn_half, upstream, attn_raw, 5
    )
    output_product = lax.dot_general(
        attended, attn_full, (((0,), (0,)), ((), ())), preferred_element_type=jnp.float32
    )
    output_weight_grad = lax.psum_scatter(
        output_product.astype(jnp.bfloat16), "gy", scatter_dimension=1, tiled=True
    ).astype(jnp.float32)
    attended_grad = lax.dot_general(
        attn_full, output_full, (((1,), (1,)), ((), ())), preferred_element_type=jnp.float32
    ).astype(jnp.bfloat16)
    query_back, key_back, value_grad, projections, query_gain_part, key_gain_part = attend_back(
        last_block,
        queries,
        keys,
        values,
        attended,
        attended_grad,
        peaks,
        query_raw,
        key_raw,
        factors,
        query_gain,
        key_gain,
        tables,
        starts[None, :],
    )
    token_grad, attn_weight_grads, gain_grads = attn_in_back(
        query_back,
        key_back,
        value_grad,
        query_raw,
        key_raw,
        factors,
        projections,
        query_gain,
        key_gain,
        attn_stack,
        inputs,
        mixed_grad,
        (query_gain_part, key_gain_part, attn_gain_part, mlp_gain_part),
        6,
    )
    query_weight_grad = attn_weight_grads[:, :local_width]
    key_weight_grad = attn_weight_grads[:, local_width : 2 * local_width]
    value_weight_grad = attn_weight_grads[:, 2 * local_width :]
    query_gain_grad, key_gain_grad, attn_gain_grad, mlp_gain_grad = (gain_grads[i] for i in range(4))
    return (
        result,
        token_grad,
        query_weight_grad,
        key_weight_grad,
        value_weight_grad,
        output_weight_grad,
        gate_weight_grad,
        up_weight_grad,
        down_weight_grad,
        query_gain_grad,
        key_gain_grad,
        attn_gain_grad,
        mlp_gain_grad,
    )


def solution(mesh):
    return jax.shard_map(
        shards,
        mesh=mesh,
        in_specs=(
            P("gy", "gx"),
            P("gy", "gx"),
            P("gy", "gx"),
            P("gy", "gx"),
            P("gx", "gy"),
            P("gy", "gx"),
            P("gy", "gx"),
            P("gx", "gy"),
            P("gx"),
            P("gx"),
            P("gx"),
            P("gx"),
            P("gy", None),
            P("gy", "gx"),
        ),
        out_specs=(
            P("gy", "gx"),
            P("gy", "gx"),
            P("gy", "gx"),
            P("gy", "gx"),
            P("gy", "gx"),
            P("gx", "gy"),
            P("gy", "gx"),
            P("gy", "gx"),
            P("gx", "gy"),
            P("gx"),
            P("gx"),
            P("gx"),
            P("gx"),
        ),
        check_vma=False,
    )
```

profile of v0, /device:TPU:0, one launch (start us, length us, event | category | flops | bytes accessed | tf_op | source)
XLA Modules:
  0.0 973.5 jit_solution(9105038803147275749)
XLA Ops:
  7.2 0.0 copy-start.23
  7.2 0.0 copy-start.22
  7.2 0.0 copy-start.11
  7.2 0.0 copy-start.12
  7.2 0.0 all-gather.3.cloned.1.call-start
  7.3 1.1 fusion.3
  8.4 2.2 fusion.2
  10.6 1.1 maximum_bitcast_fusion
  11.7 0.1 pad_maximum_fusion.2.refs_1_
  11.8 0.1 pad.6.clone
  11.9 0.1 maximum_maximum_fusion.refs_3_
  12.0 0.0 copy-done.12
  12.0 104.8 %shard_map.237 = (bf16[4,2048,512]{2,1,0:T(8,128)(2,1)}, bf16[2,2048,768]{2,1,0:T(8,128)(2,1)}, bf16[512,2048]{1,0:T(8,128)(2,1)S(1)}, f32[2048,512]{1,0:T(8,128...) custom-call(bf16[2048,512]{1,0:T(8,128)(2,1)S(1)} %copy-done.11, ...), custom_call_target="tpu_custom_call" | custom-call | flops 12884901888 | bytes 33554432 | tf_op jit(solution)/shard_map/pallas_call | solution.py:1565
  116.8 0.0 copy-start
  116.8 2.0 copy-done
  118.8 1.3 copy-done.4
  120.1 1.4 copy-done.5
  121.5 0.0 all-gather.3.cloned.1.call-update
  121.5 0.0 reduce-scatter.2.cloned.1.call-start
  121.6 0.4 copy.50
  122.0 0.1 convert_reduce_fusion.1
  122.1 0.2 reduce-window.8
  122.3 0.1 select_reduce_fusion
  122.4 0.4 copy.51
  122.8 0.5 broadcast.52
  123.3 0.7 reduce.5
  124.0 0.1 slice.65
  124.1 0.1 copy.54
  124.2 0.1 slice_reduce_fusion
  124.3 0.2 convert_reduce_fusion
  124.5 3.7 fusion
  128.2 0.0 copy-start.7
  128.2 0.0 copy-start.9
  128.3 0.6 pad_maximum_fusion
  128.9 0.1 subtract_subtract_fusion.starts
  129.0 39.1 %shard_map.238 = (bf16[2048,512]{1,0:T(8,128)(2,1)}, bf16[2048,512]{1,0:T(8,128)(2,1)}, bf16[2048,512]{1,0:T(8,128)(2,1)}, f32[8,2048]{1,0:T(8,128)S(1)}) custom-call(s32[8]{0:T(128)S(1)} %and_select_fusion.1.first_block, f32[2048,512]{1,0:T(8,128)} %copy-done, f32[2048,512]{1,0:T(8,128)} %get-tuple-element.58.key_raw.refs_4_, bf16[2048,512]{1,0:T(8,128)(2,1)} %copy-done.4, ...), custom_call_target="tpu_custom_call" | custom-call | flops 2147483648 | bytes 16777216 | tf_op jit(solution)/shard_map/pallas_call | solution.py:2141
  168.1 0.6 fusion.4
  168.7 222.1 %shard_map.239 = (bf16[2048,1024]{1,0:T(8,128)(2,1)}, f32[2048,512]{1,0:T(8,128)}, bf16[4,2048,512]{2,1,0:T(8,128)(2,1)}, bf16[2048,2048]{1,0:T(8,128)(2,1)}, bf...) custom-call(bf16[2048,512]{1,0:T(8,128)(2,1)} %get-tuple-element.62., ...), custom_call_target="tpu_custom_call" | custom-call | flops 4294967296 | bytes 33554432 | tf_op jit(solution)/shard_map/pallas_call | solution.py:863
  390.8 0.0 all-gather.3.cloned.1.call-done
  390.9 118.9 %shard_map.240 = (bf16[2048,512]{1,0:T(8,128)(2,1)}, bf16[4,2048,512]{2,1,0:T(8,128)(2,1)}, f32[1,1024]{1,0:T(1,128)}, bf16[2048,2048]{1,0:T(8,128)(2,1)}, bf16[...) custom-call(bf16[4,2048,512]{2,1,0:T(8,128)(2,1)} %get-tuple-element.66.refs_0_.refs_4_, ...), custom_call_target="tpu_custom_call" | custom-call | flops 51539607552 | bytes 67108864 | tf_op jit(solution)/shard_map/pallas_call | solution.py:1101
  509.8 100.3 %shard_map.241 = (bf16[2048,2048]{1,0:T(8,128)(2,1)}, bf16[2048,2048]{1,0:T(8,128)(2,1)}, f32[256,2048]{1,0:T(8,128)}) custom-call(bf16[4,2048,512]{2,1,0:T(8,128)(2,1)} %get-tuple-element.76.refs_0_, bf16[8,1024,256]{2,1,0:T(8,128)(2,1)} %get-tuple-element.69.refs_3_.refs_1_, bf16[8,1024,256]{2,1,0:T(8,128)(2,1)} %bitcast.50, ...), custom_call_target="tpu_custom_call" | custom-call | flops 34359738368 | bytes 67108864 | tf_op jit(solution)/shard_map/pallas_call | solution.py:1736
  610.1 180.5 %shard_map.242 = (f32[2048,512]{1,0:T(8,128)}, bf16[2048,2048]{1,0:T(8,128)(2,1)}, f32[1,1024]{1,0:T(1,128)}, f32[256,2048]{1,0:T(8,128)}, f32[256,2048]{1,0:T(8,128)}, /*index=5*/bf16[1,8,256,1024]{3,2,1,0:T(8,128)(2,1)}) custom-call(bf16[2048,2048]{1,0:T(8,128)(2,1)} %get-tuple-element.80.refs_0_, bf16[2048,2048]{1,0:T(8,128)(2,1)} %get-tuple-element.81.refs_1_, ...), custom_call_target="tpu_custom_call" | custom-call | flops 68719476736 | bytes 67108864 | tf_op jit(solution)/shard_map/pallas_call | solution.py:1289
  790.6 10.1 %convolution_convert_fusion = bf16[512,2048]{1,0:T(8,128)(2,1)} fusion(bf16[2048,512]{1,0:T(8,128)(2,1)} %get-tuple-element.62.refs_0_.attended, bf16[2048,2048]{1,0:T(8,128)(2,1)} %get-tuple-element.83), kind=kOutput, calls=%fused_computation | convolution fusion | flops 4296015872 | bytes 12582912 | tf_op jit(solution)/shard_map/dot_general | solution.py:2468
  800.8 0.0 reduce-scatter.2.cloned.1.call-update
  800.8 0.0 copy-done.6
  800.8 0.0 copy-start.8
  800.8 0.0 copy-start.10
  800.8 9.5 convolution_convert_fusion.1.upstream
  810.3 51.6 %shard_map.243 = (f32[2048,512]{1,0:T(8,128)}, f32[2048,512]{1,0:T(8,128)}, bf16[2048,512]{1,0:T(8,128)(2,1)}, f32[8,2048]{1,0:T(8,128)S(1)}, f32[1,512]{1,0:T(1,128)S(1)}, /*index=5*/f32[1,512]{1,0:T(1,128)S(1)}) custom-call(s32[8]{0:T(128)S(1)} %and_select_fusion.last_block, bf16[2048,512]{1,0:T(8,128)(2,1)} %get-tuple-element.74.queries, ...), custom_call_target="tpu_custom_call" | custom-call | flops 5368709120 | bytes 33554432 | tf_op jit(solution)/shard_map/pallas_call | solution.py:2349
  861.9 0.0 copy-start.13
  861.9 0.6 copy-done.13
  862.6 0.6 copy-done.14
  863.1 0.0 copy-done.15
  863.1 86.9 %shard_map.244 = (f32[2048,512]{1,0:T(8,128)}, f32[256,1536]{1,0:T(8,128)}, f32[8,512]{1,0:T(8,128)}, bf16[1,8,256,512]{3,2,1,0:T(8,128)(2,1)}) custom-call(f32[2048,512]{1,0:T(8,128)} %get-tuple-element.85.refs_0_, f32[2048,512]{1,0:T(8,128)} %get-tuple-element.86.refs_1_, bf16[2048,512]{1,0:T(8,128)(2,1)} %get-tuple-element.87.refs_2_, ...), custom_call_target="tpu_custom_call" | custom-call | flops 25769803776 | bytes 33554432 | tf_op jit(solution)/shard_map/pallas_call | solution.py:1963
  950.0 3.0 copy.53
  953.1 0.6 fusion.5
  953.7 2.5 fusion.1
  956.2 1.9 convert_element_type.28
  958.1 1.3 copy.59
  959.5 2.1 copy.60
  961.6 1.0 copy-done.19
  962.6 1.3 copy.61
  963.9 1.0 copy-done.18
  964.9 1.3 copy.62
  (39 shorter events, 0.1 us)
Async XLA Ops:
  7.2 4.7 copy-start.23
  7.2 4.7 copy-start.22
  7.2 4.8 copy-start.11
  7.2 4.8 copy-start.12
  7.2 383.6 %all-gather.3.cloned.1.call-start = ((), (), s32[]{:S(2)}) async-start(), calls=%async_computation.2 | async-start | bytes 4718592 | tf_op jit(solution)/shard_map/all_gather | solution.py:2442
  12.0 110.0 %copy-start.20 = (s32[1,2048]{1,0:T(1,128)S(1)}, s32[1,2048]{1,0:T(1,128)}, u32[]{:S(2)}) copy-start(s32[1,2048]{1,0:T(1,128)} %param.26) | copy-start | bytes 24580
  116.8 2.0 copy-start
  118.8 1.3 copy-start.4
  120.1 1.4 copy-start.5
  121.5 834.7 %reduce-scatter.2.cloned.1.call-start = ((), (), s32[]{:S(2)}) async-start(), calls=%async_computation.1 | async-start | bytes 2359296 | tf_op jit(solution)/shard_map/reduce_scatter | solution.py:2471
  122.0 688.3 %copy-start.3 = (f32[2,2048]{0,1:T(8,128)}, f32[2,2048]{0,1:T(8,128)S(1)}, u32[]{:S(2)}) copy-start(f32[2,2048]{0,1:T(8,128)S(1)} %copy.50) | copy-start | bytes 49156
  128.2 0.8 copy-start.7
  128.2 0.8 copy-start.9
  128.9 39.2 %copy-start.1 = (f32[2048,128]{1,0:T(8,128)}, f32[2048,128]{1,0:T(8,128)S(1)}, u32[]{:S(2)}) copy-start(f32[2048,128]{1,0:T(8,128)S(1)} %get-tuple-element.184.cosine) | copy-start | bytes 3145732
  128.9 39.2 %copy-start.2 = (f32[2048,128]{1,0:T(8,128)}, f32[2048,128]{1,0:T(8,128)S(1)}, u32[]{:S(2)}) copy-start(f32[2048,128]{1,0:T(8,128)S(1)} %get-tuple-element.185.sine) | copy-start | bytes 3145732
  790.6 10.2 %copy-start.6 = (bf16[512,2048]{1,0:T(8,128)(2,1)S(1)}, bf16[512,2048]{1,0:T(8,128)(2,1)}, u32[]{:S(2)}) copy-start(bf16[512,2048]{1,0:T(8,128)(2,1)} %copy-done.5) | copy-start | bytes 6291460
  800.8 9.5 copy-start.8
  800.8 9.5 copy-start.10
  861.9 0.6 copy-start.13
  862.6 0.6 copy-start.14
  862.6 0.6 copy-start.15
  950.0 3.1 copy-start.21
  950.0 8.1 copy-start.17
  956.2 3.3 copy-start.16
  959.5 3.1 copy-start.19
  962.6 2.3 copy-start.18
Sparse Core Ops, SparseCore 0:
  121.6 85.9 all-gather.2
  800.9 66.2 reduce-scatter.1
where the time goes:
time: 982 us; the launch traced here: 974 us
  Pallas kernels  904 us (92%)
  local copies, waits for them, and re-layouts  25.8 us (3%)
  matrix products  19.6 us (2%)
  between operations  14.9 us (2%)
    pallas_call x1, Pallas kernels, attn_out(): pl.pallas_call(kernel, out_shape=[shape((length, half), LOW), shape((leng...  222 us
    pallas_call x1, Pallas kernels, mlp_back(): pl.pallas_call(kernel, out_shape=[shape((length, width), WIDE), shape((le...  181 us
    pallas_call x1, Pallas kernels, mlp_forward(): pl.pallas_call(kernel, out_shape=[shape((length, width), LOW), shape((2 *...  119 us
    pallas_call x1, Pallas kernels, gather_in(): pl.pallas_call(kernel, out_shape=[shape((2 * chips, length, width), LOW),...  105 us
    pallas_call x1, Pallas kernels, hidden_back(): pl.pallas_call(kernel, out_shape=[shape((length, inner), LOW), shape((len...  100 us
    pallas_call x1, Pallas kernels, attn_in_back(): pl.pallas_call(kernel, out_shape=[shape((length, width), WIDE), shape((sh...  86.9 us
    pallas_call x1, Pallas kernels, attend_back(): pl.pallas_call(kernel, out_shape=[shape((length, width), WIDE), shape((le...  51.6 us
    pallas_call x1, Pallas kernels, attend(): pl.pallas_call(kernel, out_shape=[shape((length, width), LOW), shape((len...  39.1 us
  transfers between devices with their start and end apart: 2, of which 0 were waited for; matrix products, arithmetic and copies ran while one was open for 2% of the time, Pallas kernels for 41%

commit v1 on v0

--- a/solution.py
+++ b/solution.py
@@ -207,15 +207,15 @@
         self.send, self.recv, self.credit = send, recv, credit
         self.slots, self.parts = slots, parts
         self.count = lax.axis_size("gy")
-        self.rows = total.shape[1] // parts
+        self.rows = total.shape[2]
 
     @staticmethod
     def scratch(rows, columns, slots, parts):
         count = lax.axis_size("gy")
         return [
-            pltpu.VMEM((2, rows, columns), WIDE),
-            pltpu.VMEM((2, rows, columns), LOW),
-            pltpu.VMEM((slots, 2, rows, columns), LOW),
+            pltpu.VMEM((2, parts, rows, columns // parts), WIDE),
+            pltpu.VMEM((2, parts, rows, columns // parts), LOW),
+            pltpu.VMEM((slots, 2, parts, rows, columns // parts), LOW),
             pltpu.SemaphoreType.DMA((count - 1, 2, parts)),
             pltpu.SemaphoreType.DMA((count - 1, 2, parts)),
             pltpu.SemaphoreType.REGULAR((2, parts)),
@@ -223,10 +223,9 @@
 
     def copy(self, way, step, part):
         place = ring_place()
-        rows = pl.ds(aligned(part * self.rows, self.rows), self.rows)
         return remote(
-            self.sums.at[way, rows],
-            self.land.at[lax.rem(step, self.slots), way, rows],
+            self.sums.at[way, part],
+            self.land.at[lax.rem(step, self.slots), way, part],
             self.send.at[step, way, part],
             self.recv.at[step, way, part],
             {"gy": ring_device(place + 1 - 2 * way)},
@@ -245,20 +244,17 @@
         last = self.count - 1
         tile = min(self.rows, 32)
 
-        @pl.when(part == 0)
-        def _():
-            for way in range(2):
-                self.product(way, step)
-
         for way in range(2):
-            base = part * self.rows
+            self.product(way, step, part)
+
+        for way in range(2):
 
             slot = lax.rem(step - 1 + self.slots, self.slots)
 
             def over(body):
                 @pl.loop(0, self.rows // tile)
                 def _(index):
-                    body(pl.ds(aligned(base + index * tile, tile), tile))
+                    body(pl.ds(aligned(index * tile, tile), tile))
 
             @pl.when(step >= 1)
             def _():
@@ -271,22 +267,22 @@
             @pl.when(step == 0)
             def _():
                 def first(rows):
-                    self.sums[way, rows] = self.total[way, rows].astype(LOW)
+                    self.sums[way, part, rows] = self.total[way, part, rows].astype(LOW)
 
                 over(first)
 
             @pl.when((step >= 1) & (step < last))
             def _():
                 def more(rows):
-                    summed = self.total[way, rows] + self.land[slot, way, rows].astype(WIDE)
-                    self.sums[way, rows] = summed.astype(LOW)
+                    arrived = self.land[slot, way, part, rows].astype(WIDE)
+                    self.sums[way, part, rows] = (self.total[way, part, rows] + arrived).astype(LOW)
 
                 over(more)
 
             @pl.when(step == last)
             def _():
                 def final(rows):
-                    self.total[way, rows] += self.land[slot, way, rows].astype(WIDE)
+                    self.total[way, part, rows] += self.land[slot, way, part, rows].astype(WIDE)
 
                 over(final)
 
@@ -341,7 +337,7 @@
             pltpu.VMEM((1, rows, half), LOW),
             pltpu.VMEM((2, rows, half), LOW),
             pltpu.VMEM((2, rows, half), LOW),
-            pltpu.VMEM((LAG + 2, chips, rows, width) if scatter else (LAG + 2, rows, half), LOW),
+            pltpu.VMEM((LAG + 1, chips, rows, width) if scatter else (LAG + 1, rows, half), LOW),
             pltpu.VMEM((chips - 1, rows, part), LOW),
             pltpu.VMEM((rows, part), WIDE),
             pltpu.SemaphoreType.DMA((2, chunks)),
@@ -367,7 +363,7 @@
         )
 
     def cross_copy(self, shift, chunk):
-        source = self.cross.at[lax.rem(chunk, LAG + 2)]
+        source = self.cross.at[lax.rem(chunk, LAG + 1)]
         if self.scatter:
             block = lax.rem(chip_here() + shift, self.chips)
             source = source.at[block]
@@ -399,13 +395,13 @@
             ).astype(LOW)
 
     def core_sum(self, chunk):
-        slot, place = lax.rem(chunk, 2), lax.rem(chunk, LAG + 2)
+        slot, place = lax.rem(chunk, 2), lax.rem(chunk, LAG + 1)
         self.core_copy(chunk).wait_recv()
 
-        @pl.when(chunk >= LAG + 2)
+        @pl.when(chunk >= LAG + 1)
         def _():
             for shift in range(1, self.chips):
-                self.cross_copy(shift, chunk - LAG - 2).wait_send()
+                self.cross_copy(shift, chunk - LAG - 1).wait_send()
 
         @pl.loop(0, self.rows // 32)
         def _(index):
@@ -434,7 +430,7 @@
             self.cross_stage_copy(shift, chunk).start()
 
     def cross_sum(self, chunk):
-        place = lax.rem(chunk, LAG + 2)
+        place = lax.rem(chunk, LAG + 1)
         for shift in range(1, self.chips):
             self.cross_stage_copy(shift, chunk).wait()
 
@@ -452,7 +448,7 @@
     def end(self, chunks):
         for chunk in (chunks - 2, chunks - 1):
             self.core_copy(chunk).wait_send()
-        for chunk in range(chunks - LAG - 2, chunks):
+        for chunk in range(chunks - LAG - 1, chunks):
             for shift in range(1, self.chips):
                 self.cross_copy(shift, chunk).wait_send()
 
@@ -465,14 +461,14 @@
     def scratch(rows, chunks):
         return [
             pltpu.VMEM((2, rows, STATS), WIDE),
-            pltpu.VMEM((chunks, rows, STATS), WIDE),
+            pltpu.VMEM((2, rows, STATS), WIDE),
             pltpu.SemaphoreType.DMA((2, chunks)),
         ]
 
     def copy(self, chunk):
         return remote(
             self.mine.at[lax.rem(chunk, 2)],
-            self.land.at[chunk],
+            self.land.at[lax.rem(chunk, 2)],
             self.sems.at[0, chunk],
             self.sems.at[1, chunk],
             {"gx": other_core()},
@@ -488,7 +484,7 @@
         self.mine[lax.rem(chunk, 2), rows] = jnp.where(lane < STATS // 2, first, second)
 
     def get(self, chunk, rows):
-        total = self.mine[lax.rem(chunk, 2), rows] + self.land[chunk, rows]
+        total = self.mine[lax.rem(chunk, 2), rows] + self.land[lax.rem(chunk, 2), rows]
         return (total[:, :1], total[:, STATS // 2 : STATS // 2 + 1])
 
     def end(self, chunks):
@@ -601,16 +597,19 @@
 def schedule(chunks, reduce, multiply, fetch, sums, finish, event=None, events=0, prepare=None):
     steps = chunks + 1 + LAG
 
-    def iteration(step):
+    def ring_events(place):
         if event is not None:
-            low = lax.div(step * events, steps)
-            high = lax.div((step + 1) * events, steps)
+            low = lax.div(place * events, 2 * steps)
+            high = lax.div((place + 1) * events, 2 * steps)
 
             def some(index, carry):
                 event(index)
                 return carry
 
             lax.fori_loop(low, high, some, 0)
+
+    def iteration(step):
+        ring_events(2 * step)
 
         @pl.when((step >= LAG) & (step < chunks + LAG))
         def _():
@@ -627,6 +626,8 @@
             reduce.produce(step, lambda place: multiply(step, place))
             reduce.core_sum(step)
 
+        ring_events(2 * step + 1)
+
         @pl.when(step >= 1 + LAG)
         def _():
             finish(step - 1 - LAG)
@@ -656,7 +657,7 @@
     def scratch(length, shard):
         return [
             pltpu.VMEM((length, shard), LOW),
-            pltpu.VMEM((shard, length), LOW),
+            pltpu.VMEM((2, shard, length), LOW),
             pltpu.SemaphoreType.DMA((1,)),
         ]
 
@@ -668,7 +669,7 @@
 
     def take(self, ring, way, step):
         self.copy(ring.owner(way, step)).wait()
-        self.turned[...] = self.left[...].T
+        self.turned[way] = self.left[...].T
         if way == 0:
             self.copy(ring.owner(1, step)).start()
         else:
@@ -1131,7 +1132,8 @@
     chunks = count
     rows = length // chunks
     shard = D // count
-    slots, parts = 2, 2
+    slots, parts = 2, 4
+    piece = inner // parts
 
     groups = [
         Reduce.scratch(rows, chunks, width, False),
@@ -1144,7 +1146,7 @@
             pltpu.SemaphoreType.DMA((chips,)),
             pltpu.SemaphoreType.DMA((2,)),
             pltpu.SemaphoreType.DMA((1,)),
-            pltpu.SemaphoreType.DMA((2,)),
+            pltpu.SemaphoreType.DMA((2, parts)),
         ],
         Columns.scratch(length, shard),
         [
@@ -1175,20 +1177,19 @@
         up_buf, raw_buf, up_sems, raw_sems, mixed_sems, out_sems = scratch[4]
         left = Columns(inputs, shard, *scratch[5])
 
-        def product(way, step):
-            left.take(ring, way, step)
-            tile = 512
-
-            @pl.when(step == 0)
+        def product(way, step, part):
+            @pl.when(part == 0)
+            def _():
+                left.take(ring, way, step)
+
+            @pl.when((part == 0) & (step == 0))
             def _():
                 grad_copies[way].wait()
 
-            @pl.loop(0, inner // tile)
-            def _(index):
-                columns = pl.ds(aligned(index * tile, tile), tile)
-                total[way, :, columns] = jnp.dot(
-                    left.turned[...], grads[way, :, columns], preferred_element_type=WIDE
-                )
+            columns = pl.ds(aligned(part * piece, piece), piece)
+            total[way, part] = jnp.dot(
+                left.turned[way], grads[way, :, columns], preferred_element_type=WIDE
+            )
 
         ring = RingScatter(
             product, total, summed, land, ring_send, ring_recv, credit, slots, parts
@@ -1273,8 +1274,13 @@
 
         schedule(chunks, reduce, multiply, fetch, sums, finish, ring.event, ring.events, prepare)
         writes = [
-            pltpu.make_async_copy(total.at[way], (gate_out, up_out)[way], out_sems.at[way])
+            pltpu.make_async_copy(
+                total.at[way, part],
+                (gate_out, up_out)[way].at[:, part * piece : (part + 1) * piece],
+                out_sems.at[way, part],
+            )
             for way in range(2)
+            for part in range(parts)
         ]
         for item in writes:
             item.start()
@@ -1593,7 +1599,8 @@
     rows = length // chunks
     shard = D // count
     side = inner // 2
-    slots, parts = 3, 2
+    slots, parts = 3, 4
+    piece = side // parts
     down_rows = down_first.shape[1]
     tile = min(512, inner)
 
@@ -1604,7 +1611,7 @@
             pltpu.VMEM((2, 2, rows, inner), LOW),
             pltpu.SemaphoreType.DMA((2, 2)),
             pltpu.SemaphoreType.DMA((2, 2)),
-            pltpu.SemaphoreType.DMA((2,)),
+            pltpu.SemaphoreType.DMA((2, parts)),
             pltpu.VMEM((count, shard, length), LOW),
         ],
         [
@@ -1623,22 +1630,17 @@
         total, summed, land, ring_send, ring_recv, credit = scratch[0]
         given, made, given_sems, made_sems, out_sems, turned = scratch[1]
 
-        def product(way, step):
+        def product(way, step, part):
             owner = ring.owner(way, step)
 
-            @pl.when((step < count // 2) | (step == count - 1))
+            @pl.when((part == 0) & ((step < count // 2) | (step == count - 1)))
             def _():
                 turned[owner] = grad[:, pl.ds(aligned(owner * shard, shard), shard)].T
 
-            size = min(512, side)
-
-            @pl.loop(0, side // size)
-            def _(index):
-                at = pl.ds(aligned(index * size, size), size)
-                take_at = pl.ds(aligned(way * side + index * size, size), size)
-                total[way, :, at] = jnp.dot(
-                    turned[owner], hidden[:, take_at], preferred_element_type=WIDE
-                )
+            columns = pl.ds(aligned(way * side + part * piece, piece), piece)
+            total[way, part] = jnp.dot(
+                turned[owner], hidden[:, columns], preferred_element_type=WIDE
+            )
 
         ring = RingScatter(
             product, total, summed, land, ring_send, ring_recv, credit, slots, parts
@@ -1678,9 +1680,6 @@
 
         def iteration(step):
             slot = lax.rem(step, 2)
-            for part in range(parts):
-                ring.event(step * parts + part)
-
             @pl.when(step + 1 < chunks)
             def _():
                 for item in load(step + 1):
@@ -1694,20 +1693,20 @@
             for item in load(step):
                 item.wait()
 
-            @pl.when(step == 0)
-            def _():
-                for item in weight_copies:
-                    item.wait()
+            each = parts // (inner // tile)
 
             @pl.loop(0, inner // tile)
             def _(index):
+                for which in range(each):
+                    ring.event(step * parts + index * each + which)
+
+                @pl.when((step == 0) & (index == 0))
+                def _():
+                    for item in weight_copies:
+                        item.wait()
+
                 at = pl.ds(aligned(index * tile, tile), tile)
-                hidden_grad = lax.dot_general(
-                    grad[row_slice(step, rows)],
-                    weight[at],
-                    (((1,), (1,)), ((), ())),
-                    preferred_element_type=WIDE,
-                )
+                hidden_grad = nt(grad[row_slice(step, rows)], weight[at])
                 for which in range(2):
                     made[slot, which, :, at] = (
                         hidden_grad * given[slot, which, :, at].astype(WIDE)
@@ -1719,9 +1718,12 @@
         loop(chunks, iteration)
         writes = [
             pltpu.make_async_copy(
-                total.at[way], weight_grad.at[:, way * side : (way + 1) * side], out_sems.at[way]
+                total.at[way, part],
+                weight_grad.at[:, way * side + part * piece : way * side + (part + 1) * piece],
+                out_sems.at[way, part],
             )
             for way in range(2)
+            for part in range(parts)
         ]
         for item in writes:
             item.start()
@@ -1775,8 +1777,8 @@
     rows = length // chunks
     shard = D // count
     side = columns // 2
-    slots, parts = count - 1, 2
-    tile = 256 if side % 256 == 0 else 128
+    slots, parts = count - 1, 3
+    piece = side // parts
 
     groups = [
         Reduce.scratch(rows, chunks, width, True),
@@ -1792,7 +1794,7 @@
             pltpu.SemaphoreType.DMA((2,)),
             pltpu.SemaphoreType.DMA((1,)),
             pltpu.SemaphoreType.DMA((2,)),
-            pltpu.SemaphoreType.DMA((2,)),
+            pltpu.SemaphoreType.DMA((2, parts)),
         ],
         Columns.scratch(length, shard),
         Total.scratch(length),
@@ -1817,16 +1819,15 @@
         left = Columns(inputs, shard, *scratch[3])
         total_sum = Total(*scratch[4])
 
-        def product(way, step):
-            left.take(ring, way, step)
-
-            @pl.loop(0, side // tile)
-            def _(index):
-                at = pl.ds(aligned(index * tile, tile), tile)
-                take_at = pl.ds(aligned(way * side + index * tile, tile), tile)
-                total[way, :, at] = jnp.dot(
-                    left.turned[...], grads[:, take_at], preferred_element_type=WIDE
-                )
+        def product(way, step, part):
+            @pl.when(part == 0)
+            def _():
+                left.take(ring, way, step)
+
+            columns = pl.ds(aligned(way * side + part * piece, piece), piece)
+            total[way, part] = jnp.dot(
+                left.turned[way], grads[:, columns], preferred_element_type=WIDE
+            )
 
         ring = RingScatter(
             product, total, summed, land, ring_send, ring_recv, credit, slots, parts
@@ -1941,9 +1942,12 @@
         schedule(chunks, reduce, multiply, fetch, sums, finish, ring.event, ring.events, prepare)
         writes = [
             pltpu.make_async_copy(
-                total.at[way], weight_grad.at[:, way * side : (way + 1) * side], out_sems.at[way]
+                total.at[way, part],
+                weight_grad.at[:, way * side + part * piece : way * side + (part + 1) * piece],
+                out_sems.at[way, part],
             )
             for way in range(2)
+            for part in range(parts)
         ]
         for item in writes:
             item.start()
@@ -2051,46 +2055,18 @@
         attended,
         peaks,
         peak_columns,
-        given,
-        held_values,
-        given_sems,
-        value_sem,
     ):
-        def load(index):
-            slot, at = lax.rem(index, 2), row_slice(index, BLOCK)
-            return [
-                pltpu.make_async_copy(
-                    source.at[at], given.at[slot, which], given_sems.at[slot, which]
-                )
-                for which, source in enumerate((query_raw, key_raw))
-            ]
-
-        value_copy = pltpu.make_async_copy(values, held_values, value_sem.at[0])
-        for item in load(0):
-            item.start()
-        value_copy.start()
-
-        def norm_block(index):
+        @pl.loop(0, length // BLOCK)
+        def _(index):
             at = row_slice(index, BLOCK)
-            slot = lax.rem(index, 2)
-
-            @pl.when(index + 1 < length // BLOCK)
-            def _():
-                for item in load(index + 1):
-                    item.start()
-
-            for item in load(index):
-                item.wait()
             cos, sin = cosine[at], sine[at]
-            for which, (gain, out) in enumerate(((query_gain, queries), (key_gain, keys))):
+            pairs = ((query_raw, query_gain, queries), (key_raw, key_gain, keys))
+            for which, (raw, gain, out) in enumerate(pairs):
                 factor = factors[at, which : which + 1]
                 for head in range(heads):
                     columns = head_columns(head)
-                    normed = given[slot, which, :, columns] * factor * gain[:, columns]
+                    normed = raw[at, columns] * factor * gain[:, columns]
                     out[at, columns] = turn(normed, cos, sin).astype(LOW)
-
-        loop(length // BLOCK, norm_block)
-        value_copy.wait()
 
         lane = lax.broadcasted_iota(jnp.int32, (BLOCK, LANES), 1)
         row_index = lax.broadcasted_iota(jnp.int32, (BLOCK, BLOCK), 0)
@@ -2115,7 +2091,7 @@
                     shrink = jnp.exp2(peak - higher)
                     total = total * shrink + jnp.sum(raised, axis=1, keepdims=True)
                     rows = rows * shrink + jnp.dot(
-                        raised.astype(LOW), held_values[there, columns], preferred_element_type=WIDE
+                        raised.astype(LOW), values[there, columns], preferred_element_type=WIDE
                     )
                     made.append((higher, total, rows))
                 return tuple(made)
@@ -2146,15 +2122,9 @@
             shape((length, width), LOW),
             shape((8, length), WIDE),
         ],
-        in_specs=[smem] + [HBM] * 3 + [VMEM] * 6,
+        in_specs=[smem] + [VMEM] * 9,
         out_specs=[VMEM] * 4,
-        scratch_shapes=[
-            pltpu.VMEM((length, LANES), WIDE),
-            pltpu.VMEM((2, 2, BLOCK, width), WIDE),
-            pltpu.VMEM((length, width), LOW),
-            pltpu.SemaphoreType.DMA((2, 2)),
-            pltpu.SemaphoreType.DMA((1,)),
-        ],
+        scratch_shapes=[pltpu.VMEM((length, LANES), WIDE)],
         compiler_params=pltpu.CompilerParams(vmem_limit_bytes=48 * MIB),
         cost_estimate=pl.CostEstimate(
             flops=2 * length * MAX_LEN * width,
@@ -2210,25 +2180,7 @@
         value_sum,
         columns_scratch,
         deltas,
-        held_query,
-        held_key,
-        made,
-        load_sems,
-        made_sems,
     ):
-        loads = [
-            pltpu.make_async_copy(query_raw, held_query, load_sems.at[0]),
-            pltpu.make_async_copy(key_raw, held_key, load_sems.at[1]),
-        ]
-        for item in loads:
-            item.start()
-
-        def store(index, out):
-            slot = lax.rem(index, 2)
-            return pltpu.make_async_copy(
-                made.at[slot], out.at[row_slice(index, BLOCK)], made_sems.at[slot]
-            )
-
         lane = lax.broadcasted_iota(jnp.int32, (BLOCK, LANES), 1)
         query_gain_grad[...] = jnp.zeros_like(query_gain_grad)
         key_gain_grad[...] = jnp.zeros_like(key_gain_grad)
@@ -2252,23 +2204,16 @@
         row_index = lax.broadcasted_iota(jnp.int32, (BLOCK, BLOCK), 0)
         column_index = lax.broadcasted_iota(jnp.int32, (BLOCK, BLOCK), 1)
 
-        def turn_back(index, summed, raw, gain, factor, out, gain_grad):
-            at, slot = row_slice(index, BLOCK), lax.rem(index, 2)
-
-            @pl.when(index >= 2)
-            def _():
-                store(index - 2, out).wait()
-
+        def turn_back(at, summed, raw, gain, factor, out, gain_grad):
             cos, sin = cosine[at], sine[at]
             share = jnp.zeros((BLOCK, 1), WIDE)
             for head in range(heads):
                 columns = head_columns(head)
                 normed = turn(summed(head) * SCALE, cos, -sin)
-                made[slot, :, columns] = normed
+                out[at, columns] = normed
                 weighed = normed * raw[at, columns]
                 share += jnp.sum(gain[:, columns] * weighed, axis=1, keepdims=True)
                 gain_grad[:, columns] += jnp.sum(weighed * factor, axis=0, keepdims=True)
-            store(index, out).start()
             return share
 
         def key_block(index):
@@ -2305,15 +2250,10 @@
 
             lax.fori_loop(index, last_block[index] + 1, query_block, 0)
             value_out[at] = value_sum[...].astype(LOW)
-
-            @pl.when(index == 0)
-            def _():
-                loads[1].wait()
-
             share = turn_back(
-                index,
+                at,
                 lambda head: key_sum[:, head_columns(head)],
-                held_key,
+                key_raw,
                 key_gain,
                 factors[at, 1:2],
                 key_out,
@@ -2322,16 +2262,13 @@
             columns_scratch[at] = jnp.where(lane == 1, share, 0.0)
 
         loop(length // BLOCK, key_block)
-        for index in (length // BLOCK - 2, length // BLOCK - 1):
-            store(index, key_out).wait()
-        loads[0].wait()
 
         def finish(index):
             at = row_slice(index, BLOCK)
             share = turn_back(
-                index,
+                at,
                 lambda head: query_sum[at, head_columns(head)],
-                held_query,
+                query_raw,
                 query_gain,
                 factors[at, 0:1],
                 query_out,
@@ -2340,8 +2277,6 @@
             columns_scratch[at] += jnp.where(lane == 0, share, 0.0)
 
         loop(length // BLOCK, finish)
-        for index in (length // BLOCK - 2, length // BLOCK - 1):
-            store(index, query_out).wait()
         projections[...] = columns_scratch[...].T[:8]
 
     shape = jax.ShapeDtypeStruct
@@ -2356,19 +2291,14 @@
             shape((1, width), WIDE),
             shape((1, width), WIDE),
         ],
-        in_specs=[smem] + [VMEM] * 6 + [HBM] * 2 + [VMEM] * 6,
-        out_specs=[HBM] * 2 + [VMEM] * 4,
+        in_specs=[smem] + [VMEM] * 14,
+        out_specs=[VMEM] * 6,
         scratch_shapes=[
             pltpu.VMEM((length, width), WIDE),
             pltpu.VMEM((BLOCK, width), WIDE),
             pltpu.VMEM((BLOCK, width), WIDE),
             pltpu.VMEM((length, LANES), WIDE),
             pltpu.VMEM((8, length), WIDE),
-            pltpu.VMEM((length, width), WIDE),
-            pltpu.VMEM((length, width), WIDE),
-            pltpu.VMEM((2, BLOCK, width), WIDE),
-            pltpu.SemaphoreType.DMA((2,)),
-            pltpu.SemaphoreType.DMA((2,)),
         ],
         compiler_params=pltpu.CompilerParams(vmem_limit_bytes=52 * MIB),
         cost_estimate=pl.CostEstimate(

time: 982 us -> 987 us (level)
    pallas_call x1, Pallas kernels: 86.9 us -> 100 us  [attn_in_back(): pl.pallas_call(kernel, out_shape=[shape((length, width), WIDE), shape((sh...]
  transfers between devices with their start and end apart: 2 -> 2, of which waited for: 0 -> 0; matrix products, arithmetic and copies ran while one was open for 2% -> 2% of each run, Pallas kernels for 41% -> 42%
where the time goes in v1:
time: 987 us; the launch traced here: 980 us
  Pallas kernels  910 us (92%)
  local copies, waits for them, and re-layouts  25.8 us (3%)
  matrix products  19.6 us (2%)
  between operations  14.8 us (1%)
    pallas_call x1, Pallas kernels, attn_out(): pl.pallas_call(kernel, out_shape=[shape((length, half), LOW), shape((leng...  226 us
    pallas_call x1, Pallas kernels, mlp_back(): pl.pallas_call(kernel, out_shape=[shape((length, width), WIDE), shape((le...  180 us
    pallas_call x1, Pallas kernels, mlp_forward(): pl.pallas_call(kernel, out_shape=[shape((length, width), LOW), shape((2 *...  119 us
    pallas_call x1, Pallas kernels, gather_in(): pl.pallas_call(kernel, out_shape=[shape((2 * chips, length, width), LOW),...  105 us
    pallas_call x1, Pallas kernels, attn_in_back(): pl.pallas_call(kernel, out_shape=[shape((length, width), WIDE), shape((sh...  100 us
    pallas_call x1, Pallas kernels, hidden_back(): pl.pallas_call(kernel, out_shape=[shape((length, inner), LOW), shape((len...  97.6 us
    pallas_call x1, Pallas kernels, attend_back(): pl.pallas_call(kernel, out_shape=[shape((length, width), WIDE), shape((le...  48.1 us
    pallas_call x1, Pallas kernels, attend(): pl.pallas_call(kernel, out_shape=[shape((length, width), LOW), shape((len...  34.9 us
  transfers between devices with their start and end apart: 2, of which 0 were waited for; matrix products, arithmetic and copies ran while one was open for 2% of the time, Pallas kernels for 42%

profile of v1, /device:TPU:0, one launch (start us, length us, event | category | flops | bytes accessed | tf_op | source)
XLA Modules:
  0.0 979.7 jit_solution(2840009674823813770)
XLA Ops:
  7.2 0.0 all-gather.3.cloned.1.call-start
  7.3 1.1 fusion.3
  8.4 2.2 fusion.2
  10.6 1.1 maximum_bitcast_fusion
  11.7 0.1 pad_maximum_fusion.2.refs_1_
  11.8 0.1 pad.6.clone
  11.9 0.0 copy-done.23
  11.9 0.1 maximum_maximum_fusion.refs_3_
  12.0 0.0 copy-done.11
  12.0 104.8 %shard_map.237 = (bf16[4,2048,512]{2,1,0:T(8,128)(2,1)}, bf16[2,2048,768]{2,1,0:T(8,128)(2,1)}, bf16[512,2048]{1,0:T(8,128)(2,1)S(1)}, f32[2048,512]{1,0:T(8,128...) custom-call(bf16[2048,512]{1,0:T(8,128)(2,1)S(1)} %copy-done.11, ...), custom_call_target="tpu_custom_call" | custom-call | flops 12884901888 | bytes 33554432 | tf_op jit(solution)/shard_map/pallas_call | solution.py:1571
  116.8 0.0 copy-start
  116.8 2.0 copy-done
  118.8 1.3 copy-done.4
  120.1 1.4 copy-done.5
  121.5 0.0 all-gather.3.cloned.1.call-update
  121.5 0.0 reduce-scatter.2.cloned.1.call-start
  121.6 0.4 copy.50
  122.0 0.1 convert_reduce_fusion.1
  122.1 0.2 reduce-window.8
  122.3 0.1 select_reduce_fusion
  122.4 0.4 copy.51
  122.8 0.5 broadcast.52
  123.3 0.7 reduce.5
  124.0 0.1 slice.65
  124.1 0.1 copy.54
  124.2 0.1 slice_reduce_fusion
  124.3 0.2 convert_reduce_fusion
  124.5 3.7 fusion
  128.2 0.0 copy-start.7
  128.2 0.0 copy-start.9
  128.3 0.6 pad_maximum_fusion
  128.9 0.1 subtract_subtract_fusion.starts
  129.0 0.0 copy-done.7
  129.0 0.0 copy-done.9
  129.0 34.9 %shard_map.238 = (bf16[2048,512]{1,0:T(8,128)(2,1)}, bf16[2048,512]{1,0:T(8,128)(2,1)}, bf16[2048,512]{1,0:T(8,128)(2,1)}, f32[8,2048]{1,0:T(8,128)S(1)}) custom-call(s32[8]{0:T(128)S(1)} %and_select_fusion.1.first_block, f32[2048,512]{1,0:T(8,128)} %copy-done, f32[2048,512]{1,0:T(8,128)} %get-tuple-element.58.key_raw.refs_4_, bf16[2048,512]{1,0:T(8,128)(2,1)} %copy-done.4, ...), custom_call_target="tpu_custom_call" | custom-call | flops 2147483648 | bytes 16777216 | tf_op jit(solution)/shard_map/pallas_call | solution.py:2117
  163.9 0.0 copy-done.2
  164.0 0.6 fusion.4
  164.6 226.3 %shard_map.239 = (bf16[2048,1024]{1,0:T(8,128)(2,1)}, f32[2048,512]{1,0:T(8,128)}, bf16[4,2048,512]{2,1,0:T(8,128)(2,1)}, bf16[2048,2048]{1,0:T(8,128)(2,1)}, bf...) custom-call(bf16[2048,512]{1,0:T(8,128)(2,1)} %get-tuple-element.62., ...), custom_call_target="tpu_custom_call" | custom-call | flops 4294967296 | bytes 33554432 | tf_op jit(solution)/shard_map/pallas_call | solution.py:864
  390.8 0.0 all-gather.3.cloned.1.call-done
  390.9 118.9 %shard_map.240 = (bf16[2048,512]{1,0:T(8,128)(2,1)}, bf16[4,2048,512]{2,1,0:T(8,128)(2,1)}, f32[1,1024]{1,0:T(1,128)}, bf16[2048,2048]{1,0:T(8,128)(2,1)}, bf16[...) custom-call(bf16[4,2048,512]{2,1,0:T(8,128)(2,1)} %get-tuple-element.66.refs_0_.refs_4_, ...), custom_call_target="tpu_custom_call" | custom-call | flops 51539607552 | bytes 67108864 | tf_op jit(solution)/shard_map/pallas_call | solution.py:1102
  509.8 97.6 %shard_map.241 = (bf16[2048,2048]{1,0:T(8,128)(2,1)}, bf16[2048,2048]{1,0:T(8,128)(2,1)}, f32[256,2048]{1,0:T(8,128)}) custom-call(bf16[4,2048,512]{2,1,0:T(8,128)(2,1)} %get-tuple-element.76.refs_0_, bf16[8,1024,256]{2,1,0:T(8,128)(2,1)} %get-tuple-element.69.refs_3_.refs_1_, bf16[8,1024,256]{2,1,0:T(8,128)(2,1)} %bitcast.50, ...), custom_call_target="tpu_custom_call" | custom-call | flops 34359738368 | bytes 67108864 | tf_op jit(solution)/shard_map/pallas_call | solution.py:1738
  607.4 179.5 %shard_map.242 = (f32[2048,512]{1,0:T(8,128)}, bf16[2048,2048]{1,0:T(8,128)(2,1)}, f32[1,1024]{1,0:T(1,128)}, f32[256,2048]{1,0:T(8,128)}, f32[256,2048]{1,0:T(8,128)}, /*index=5*/bf16[1,8,256,1024]{3,2,1,0:T(8,128)(2,1)}) custom-call(bf16[2048,2048]{1,0:T(8,128)(2,1)} %get-tuple-element.80.refs_0_, bf16[2048,2048]{1,0:T(8,128)(2,1)} %get-tuple-element.81.refs_1_, ...), custom_call_target="tpu_custom_call" | custom-call | flops 68719476736 | bytes 67108864 | tf_op jit(solution)/shard_map/pallas_call | solution.py:1295
  786.9 10.1 %convolution_convert_fusion = bf16[512,2048]{1,0:T(8,128)(2,1)} fusion(bf16[2048,512]{1,0:T(8,128)(2,1)} %get-tuple-element.62.refs_0_.attended, bf16[2048,2048]{1,0:T(8,128)(2,1)} %get-tuple-element.83), kind=kOutput, calls=%fused_computation | convolution fusion | flops 4296015872 | bytes 12582912 | tf_op jit(solution)/shard_map/dot_general | solution.py:2398
  797.0 0.0 reduce-scatter.2.cloned.1.call-update
  797.1 0.0 copy-start.8
  797.1 0.0 copy-start.10
  797.1 9.5 convolution_convert_fusion.1.upstream
  806.6 48.1 %shard_map.243 = (f32[2048,512]{1,0:T(8,128)}, f32[2048,512]{1,0:T(8,128)}, bf16[2048,512]{1,0:T(8,128)(2,1)}, f32[8,2048]{1,0:T(8,128)S(1)}, f32[1,512]{1,0:T(1,128)S(1)}, /*index=5*/f32[1,512]{1,0:T(1,128)S(1)}) custom-call(s32[8]{0:T(128)S(1)} %and_select_fusion.last_block, bf16[2048,512]{1,0:T(8,128)(2,1)} %get-tuple-element.74.queries, ...), custom_call_target="tpu_custom_call" | custom-call | flops 5368709120 | bytes 33554432 | tf_op jit(solution)/shard_map/pallas_call | solution.py:2284
  854.7 0.6 copy-done.13
  855.3 0.6 copy-done.14
  855.9 0.0 copy-done.15
  855.9 100.2 %shard_map.244 = (f32[2048,512]{1,0:T(8,128)}, f32[256,1536]{1,0:T(8,128)}, f32[8,512]{1,0:T(8,128)}, bf16[1,8,256,512]{3,2,1,0:T(8,128)(2,1)}) custom-call(f32[2048,512]{1,0:T(8,128)} %get-tuple-element.85.refs_0_, f32[2048,512]{1,0:T(8,128)} %get-tuple-element.86.refs_1_, bf16[2048,512]{1,0:T(8,128)(2,1)} %get-tuple-element.87.refs_2_, ...), custom_call_target="tpu_custom_call" | custom-call | flops 25769803776 | bytes 33554432 | tf_op jit(solution)/shard_map/pallas_call | solution.py:1967
  956.2 0.0 copy-start.21
  956.2 0.0 copy-start.17
  956.2 3.0 copy.53
  959.2 0.6 fusion.5
  959.8 2.5 fusion.1
  962.4 1.9 convert_element_type.28
  964.3 1.3 copy.59
  965.6 2.1 copy.60
  967.7 1.0 copy-done.19
  968.7 1.3 copy.61
  970.0 1.0 copy-done.18
  971.1 1.3 copy.62
  (39 shorter events, 0.1 us)
Async XLA Ops:
  7.2 4.7 copy-start.23
  7.2 4.7 copy-start.22
  7.2 4.8 copy-start.11
  7.2 4.8 copy-start.12
  7.2 383.6 %all-gather.3.cloned.1.call-start = ((), (), s32[]{:S(2)}) async-start(), calls=%async_computation.2 | async-start | bytes 4718592 | tf_op jit(solution)/shard_map/all_gather | solution.py:2372
  12.0 110.0 %copy-start.20 = (s32[1,2048]{1,0:T(1,128)S(1)}, s32[1,2048]{1,0:T(1,128)}, u32[]{:S(2)}) copy-start(s32[1,2048]{1,0:T(1,128)} %param.26) | copy-start | bytes 24580
  116.8 2.0 copy-start
  118.8 1.3 copy-start.4
  120.1 1.4 copy-start.5
  121.5 840.8 %reduce-scatter.2.cloned.1.call-start = ((), (), s32[]{:S(2)}) async-start(), calls=%async_computation.1 | async-start | bytes 2359296 | tf_op jit(solution)/shard_map/reduce_scatter | solution.py:2401
  122.0 684.6 %copy-start.3 = (f32[2,2048]{0,1:T(8,128)}, f32[2,2048]{0,1:T(8,128)S(1)}, u32[]{:S(2)}) copy-start(f32[2,2048]{0,1:T(8,128)S(1)} %copy.50) | copy-start | bytes 49156
  128.2 0.8 copy-start.7
  128.2 0.8 copy-start.9
  128.9 35.1 %copy-start.1 = (f32[2048,128]{1,0:T(8,128)}, f32[2048,128]{1,0:T(8,128)S(1)}, u32[]{:S(2)}) copy-start(f32[2048,128]{1,0:T(8,128)S(1)} %get-tuple-element.184.cosine) | copy-start | bytes 3145732
  128.9 35.1 %copy-start.2 = (f32[2048,128]{1,0:T(8,128)}, f32[2048,128]{1,0:T(8,128)S(1)}, u32[]{:S(2)}) copy-start(f32[2048,128]{1,0:T(8,128)S(1)} %get-tuple-element.185.sine) | copy-start | bytes 3145732
  786.9 10.2 %copy-start.6 = (bf16[512,2048]{1,0:T(8,128)(2,1)S(1)}, bf16[512,2048]{1,0:T(8,128)(2,1)}, u32[]{:S(2)}) copy-start(bf16[512,2048]{1,0:T(8,128)(2,1)} %copy-done.5) | copy-start | bytes 6291460
  797.1 9.5 copy-start.8
  797.1 9.5 copy-start.10
  854.7 0.6 copy-start.13
  855.3 0.6 copy-start.14
  855.3 0.6 copy-start.15
  956.2 3.1 copy-start.21
  956.2 8.1 copy-start.17
  962.4 3.3 copy-start.16
  965.6 3.1 copy-start.19
  968.7 2.3 copy-start.18
Sparse Core Ops, SparseCore 0:
  121.6 88.5 all-gather.2
  797.2 66.4 reduce-scatter.1
